TPU v7x, 32 devices: a whole 2x2x4 slice. The times are simulated.
32 devices in a mesh: hx: 2 (over x), hy: 4 (over y, core), vz: 4 (over z).
Axes of the slice: x: 2, y: 2, z: 4, core: 2. Of those that a mesh axis runs over, the one named last changes fastest.
Arguments:
- prognostic: float32 [5, 80, 4, 4, 4, 256], P(None, 'vz', None, None, 'hy', 'hx'), may hold values from -6 to 6
- metric: float32 [4, 4, 4, 256], P(None, None, 'hy', 'hx'), may hold values from 0.5 to 2
- first_flux: float32 [5, 5], replicated, may hold values from -2.5 to 2.5
- second_flux: float32 [5, 5], replicated, may hold values from -2.5 to 2.5
- neighbour_face: int32 [4, 4, 256], P(None, 'hy', 'hx'), may hold values from 0 to 3
- orientation: int32 [4, 4, 256], P(None, 'hy', 'hx'), may hold values from 0 to 1
- coupling: float32 [4, 80, 4, 4, 4, 256], P(None, None, 'vz', None, 'hy', 'hx'), may hold values from 0.1 to 1
- damping: float32 [4, 4, 4, 256], P('vz', None, 'hy', 'hx'), may hold values from 0.005 to 0.05
Outputs:
- updated: float32 [5, 80, 4, 4, 4, 256], P(None, 'vz', None, None, 'hy', 'hx')
All inputs are finite; a program needn't handle non-finite values.
Results may differ from a plain program's by a relative error of at most 0.0003.
Values sent between devices are 32-bit elements; how exact they have to be, the bound alone decides.
No kernel may reach another device: no remote copies, remote signals or barrier semaphores. Data moves between devices by JAX's collectives and lax.ppermute only.
A program may use at most 64 MiB of HBM per device.

v0:
```python
import functools

import jax
import jax.numpy as jnp
import numpy as np
from jax import lax
from jax.experimental import pallas as pl
from jax.experimental.pallas import tpu as pltpu
from jax.sharding import PartitionSpec as P

step_size = 0.05
lift_weight = 6.0
gravity_couple = 0.5
density_couple = 0.3
theta_couple = 0.4

NODES = 4
POINTS = NODES * NODES
FIELDS = 5
FACE_POINTS = ((0, 4, 8, 12), (3, 7, 11, 15), (0, 1, 2, 3), (12, 13, 14, 15))
RIM_POINTS = tuple(sorted(set(sum(FACE_POINTS, ()))))
ROWS = 8
LATE_FIELDS = (0, 1, 2, 4)
WAYS = (2, 3, 1, 0)
BACK_WAYS = (3, 2, 1, 0)


def derivative_table():
    points = np.array([-1.0, -1.0 / np.sqrt(5.0), 1.0 / np.sqrt(5.0), 1.0])
    number = points.shape[0]
    barycentric = np.ones(number)
    for source in range(number):
        for another in range(number):
            if another != source:
                barycentric[source] = barycentric[source] / (points[source] - points[another])
    matrix = np.zeros((number, number))
    for target in range(number):
        for source in range(number):
            if target != source:
                matrix[target, source] = (
                    barycentric[source] / barycentric[target] / (points[target] - points[source])
                )
        matrix[target, target] = -np.sum(matrix[target])
    return matrix


def operator_tables(lanes):
    weight = 0.5 * lift_weight
    table = derivative_table()
    table[0, 0] += weight
    table[-1, -1] -= weight
    eye = np.eye(NODES)
    along_first = np.kron(eye, table)
    along_second = np.kron(table, eye)
    ends = np.zeros(NODES)
    ends[0] = ends[-1] = 1.0
    faces = np.diag(np.kron(np.ones(NODES), ends) + np.kron(ends, np.ones(NODES)))
    first = np.zeros((POINTS, lanes))
    second = np.zeros((POINTS, lanes))
    same = np.zeros((FIELDS, POINTS, lanes))
    owner = np.full((lanes,), -1)
    for g in range(FIELDS):
        own = slice(POINTS * g, POINTS * (g + 1))
        first[:, own] = -along_first
        second[:, own] = -along_second
        same[g, :, own] = -weight * faces
        owner[own] = g
        for k in range(NODES):
            south = FIELDS * POINTS + 2 * NODES * g + k
            north = south + NODES
            second[FACE_POINTS[2][k], south] = weight
            second[FACE_POINTS[3][k], north] = -weight
            same[g, FACE_POINTS[2][k], south] = weight
            same[g, FACE_POINTS[3][k], north] = weight
            owner[south] = owner[north] = g
    tables = np.concatenate([first, second, same.reshape(FIELDS * POINTS, lanes)])
    return tables.astype(np.float32), owner


def chunks(total):
    return [min(start, total - ROWS) for start in range(0, total, ROWS)]


def partner_side(partner):
    odd = lax.rem(lax.axis_index("hy"), 2)
    return odd if partner else 1 - odd


def side_sign(side):
    return (2 * side - 1).astype(jnp.float32)


def ends(total):
    return list(range(0, total, ROWS))


def pick(values, masks, flip):
    chosen = []
    for k in range(NODES):
        row = values[FACE_POINTS[0][k]]
        for option in range(1, 4):
            row = jnp.where(masks[option], values[FACE_POINTS[option][k]], row)
        chosen.append(row)
    return [jnp.where(flip, chosen[NODES - 1 - k], chosen[k]) for k in range(NODES)]


def table_masks(face_row, flip_row, lanes):
    face = jnp.broadcast_to(face_row, (ROWS, lanes))
    flip = jnp.broadcast_to(flip_row, (ROWS, lanes))
    return [face == option for option in range(4)], flip == 1


def flux_row(f, g, matrix):
    return (matrix * FIELDS + f) * FIELDS + g


def along(fluxes, matrix, f, rows):
    total = None
    for g in range(FIELDS):
        at = flux_row(f, g, matrix)
        term = fluxes[at : at + 1, :] * rows[g]
        total = term if total is None else total + term
    return total


def side_rows(f, piece):
    number = 3 * f + piece
    return number // 4, 32 * (number % 4)


def rim_kernel(
    state_hbm,
    face_hbm,
    way_hbm,
    metric_hbm,
    tables_hbm,
    flux_hbm,
    second_hbm,
    to_other,
    state,
    neighbour_face,
    orientation,
    metric,
    tables,
    fluxes,
    column,
    speed,
    flux,
    second_flux,
    semaphores,
):
    levels = state.shape[1] // POINTS
    face = partner_side(1)
    sign = side_sign(face)
    lanes = state.shape[2]
    width = len(RIM_POINTS)
    groups = [(start, min(start + ROWS, levels)) for start in range(0, levels, ROWS)]
    small = [
        pltpu.make_async_copy(source, target, semaphores.at[place])
        for place, (source, target) in enumerate(
            (
                (flux_hbm, flux),
                (face_hbm, neighbour_face),
                (way_hbm, orientation),
                (metric_hbm, metric),
                (tables_hbm, tables),
                (second_hbm, second_flux),
            )
        )
    ]
    large = []
    for place, (low, high) in enumerate(groups):
        rows = pl.ds(low * POINTS, (high - low) * POINTS)
        large.append(
            pltpu.make_async_copy(
                state_hbm.at[:, rows, :], state.at[:, rows, :], semaphores.at[len(small) + place]
            )
        )
    for copy in small[:1] + large + small[1:]:
        copy.start()
    column[...] = jnp.zeros_like(column)
    small[0].wait()
    arrived = 0
    for piece, start in enumerate(chunks(levels)):
        while arrived < len(groups) and groups[arrived][0] < start + ROWS:
            large[arrived].wait()
            arrived += 1
        for place, point in enumerate(RIM_POINTS):
            rows = [
                state[g, pl.ds(start * POINTS + point, ROWS, stride=POINTS), :]
                for g in range(FIELDS)
            ]
            for f, out in ((3, speed), (4, column)):
                normal = (sign * flux[f, 0]) * rows[0]
                for g in range(1, FIELDS):
                    normal = normal + (sign * flux[f, g]) * rows[g]
                out[place, pl.ds(ROWS + start, ROWS), :] = rows[f] + normal
    small[1].wait()
    small[2].wait()
    end = (levels + 2) * width
    for place in range(width):
        for start in chunks(levels):
            upper = column[place, pl.ds(ROWS + start + 1, ROWS), :]
            lower = column[place, pl.ds(ROWS + start - 1, ROWS), :]
            to_other[pl.ds(start * width + place, ROWS, stride=width), :] = speed[
                place, pl.ds(ROWS + start, ROWS), :
            ] - gravity_couple * (upper - lower)
        for extra, level in ((0, 0), (1, levels - 1)):
            at = (levels + extra) * width + place
            to_other[at : at + 1, :] = column[place, ROWS + level : ROWS + level + 1, :]
    to_other[end : end + 1, :] = neighbour_face[pl.ds(face, 1), :].astype(jnp.float32)
    to_other[end + 1 : end + 2, :] = orientation[pl.ds(face, 1), :].astype(jnp.float32)
    left = to_other.shape[0] - end - 2
    to_other[end + 2 :, :] = jnp.zeros((left, lanes), jnp.float32)
    small[3].wait()
    small[4].wait()
    small[5].wait()
    for place, source in enumerate((flux, second_flux)):
        for f in range(FIELDS):
            for g in range(FIELDS):
                at = flux_row(f, g, place)
                fluxes[at : at + 1, :] = jnp.full((1, lanes), source[f, g])


def edge_kernel(state, to_sides):
    lanes = state.shape[1]
    levels = state.shape[0] // (FIELDS * POINTS)
    lane = lax.broadcasted_iota(jnp.int32, (ROWS, lanes), 1)
    packed = [jnp.zeros((ROWS, lanes), jnp.float32) for _ in range(to_sides.shape[0] // ROWS)]
    for f in range(FIELDS):
        for piece, start in enumerate(chunks(levels)):
            block, at = side_rows(f, piece)
            for place, point in enumerate(RIM_POINTS):
                row = state[pl.ds((f * levels + start) * POINTS + point, ROWS, stride=POINTS), :]
                first = at + 2 * place
                packed[block] = jnp.where(
                    lane // 2 == first // 2, pltpu.roll(row, first + 1, 1), packed[block]
                )
    for block, value in enumerate(packed):
        to_sides[block * ROWS : (block + 1) * ROWS, :] = value


def near_kernel(
    state, neighbour_face, orientation, fluxes, base, metric, half, late, column, source
):
    lanes = state.shape[1]
    levels = state.shape[0] // (FIELDS * POINTS)
    face = partner_side(0)
    sign = -side_sign(face)
    masks, flip = table_masks(
        neighbour_face[pl.ds(face, 1), :], orientation[pl.ds(face, 1), :], lanes
    )
    column[...] = jnp.zeros_like(column)
    speeds = []
    for start in chunks(levels):
        picked = []
        for g in range(FIELDS):
            values = {
                point: state[pl.ds((g * levels + start) * POINTS + point, ROWS, stride=POINTS), :]
                for point in RIM_POINTS
            }
            picked.append(pick(values, masks, flip))
        for k in range(NODES):
            rows = [picked[g][k] for g in range(FIELDS)]
            changed = [rows[f] + sign * along(fluxes, 0, f, rows) for f in range(FIELDS)]
            for place, f in enumerate(LATE_FIELDS):
                at = (place * levels + start) * NODES + k
                late[pl.ds(at, ROWS, stride=NODES), :] = changed[f]
            column[k, pl.ds(ROWS + start, ROWS), :] = changed[4]
            speeds.append(changed[3])
    for piece, start in enumerate(chunks(levels)):
        for k in range(NODES):
            upper = column[k, pl.ds(ROWS + start + 1, ROWS), :]
            lower = column[k, pl.ds(ROWS + start - 1, ROWS), :]
            source[pl.ds(start * NODES + k, ROWS, stride=NODES), :] = speeds[
                NODES * piece + k
            ] - gravity_couple * (upper - lower)
    for extra, level in ((0, 0), (1, levels - 1)):
        for k in range(NODES):
            at = (levels + extra) * NODES + k
            source[at : at + 1, :] = column[k, ROWS + level : ROWS + level + 1, :]
    half[...] = base[...]
    for start in chunks(levels + 2):
        picked = [source[pl.ds(start * NODES + k, ROWS, stride=NODES), :] for k in range(NODES)]
        add_first_side(0, start, picked, half, base, metric)


def face_kernel(partner, state, received, fluxes, *rest):
    lanes = state.shape[1]
    levels = state.shape[0] // (FIELDS * POINTS)
    at = (levels + 2) * len(RIM_POINTS)
    outs = rest[-2:]
    share = len(LATE_FIELDS) // len(outs)
    sign = side_sign(partner_side(partner))
    masks, flip = table_masks(
        received[at : at + 1, :].astype(jnp.int32),
        received[at + 1 : at + 2, :].astype(jnp.int32),
        lanes,
    )
    for start in chunks(levels):
        picked = []
        for g in range(FIELDS):
            values = {
                point: state[pl.ds((g * levels + start) * POINTS + point, ROWS, stride=POINTS), :]
                for point in RIM_POINTS
            }
            picked.append(pick(values, masks, flip))
        for place, f in enumerate(LATE_FIELDS):
            for k in range(NODES):
                normal = along(fluxes, 0, f, [picked[g][k] for g in range(FIELDS)])
                at = ((place % share) * levels + start) * NODES + k
                outs[place // share][pl.ds(at, ROWS, stride=NODES), :] = (
                    picked[f][k] + sign * normal
                )


def element_kernel(
    state,
    neighbour_face,
    orientation,
    metric,
    fluxes,
    tables,
    part,
    base,
    outer,
    operator_high,
    operator_low,
):
    levels = state.shape[0] // (FIELDS * POINTS)
    lanes = state.shape[1]
    lane = lax.broadcasted_iota(jnp.int32, (ROWS, lanes), 1)
    sides = []
    for side, (face, edge) in enumerate(((2, 0), (3, lanes - 1))):
        shift = 1 if side == 0 else lanes - 1
        row = jnp.broadcast_to(neighbour_face[face : face + 1, :], (ROWS, lanes))
        way = jnp.broadcast_to(orientation[face : face + 1, :], (ROWS, lanes))
        masks, flip = table_masks(
            pltpu.roll(row, lanes - shift, 1), pltpu.roll(way, lanes - shift, 1), lanes
        )
        sides.append((shift, edge, masks, flip))
    for f in range(FIELDS):
        for start in chunks(levels):
            q = f * levels + start
            values = {
                point: state[pl.ds(q * POINTS + point, ROWS, stride=POINTS), :]
                for point in RIM_POINTS
            }
            for side, (shift, edge, masks, flip) in enumerate(sides):
                for k, row in enumerate(pick(values, masks, flip)):
                    at = start * 8 * FIELDS + 8 * f + NODES * side + k
                    outer[pl.ds(at, ROWS, stride=8 * FIELDS), :] = jnp.where(
                        lane == edge, 0.0, pltpu.roll(row, shift, 1)
                    )
    index = lax.broadcasted_iota(jnp.int32, (1, lanes), 1)
    own_columns = FIELDS * POINTS
    owner = jnp.where(index < own_columns, index // POINTS, (index - own_columns) // 8)
    for f in range(FIELDS):
        first_row = jnp.zeros((1, lanes), jnp.float32)
        second_row = first_row
        for g in range(FIELDS):
            first, second = (flux_row(f, g, matrix) for matrix in range(2))
            first_row = jnp.where(owner == g, fluxes[first : first + 1, :], first_row)
            second_row = jnp.where(owner == g, fluxes[second : second + 1, :], second_row)
        block = (
            first_row * tables[0:POINTS, :]
            + second_row * tables[POINTS : 2 * POINTS, :]
            + tables[(2 + f) * POINTS : (3 + f) * POINTS, :]
        )
        high = block.astype(jnp.bfloat16)
        operator_high[f * POINTS : (f + 1) * POINTS, :] = high
        operator_low[f * POINTS : (f + 1) * POINTS, :] = (
            block - high.astype(jnp.float32)
        ).astype(jnp.bfloat16)
    high = operator_high[...]
    low = operator_low[...]
    scale = step_size * metric[...]
    blank = jnp.zeros((lanes - own_columns - 8 * FIELDS, lanes), jnp.float32)
    for pair in range(0, levels, 2):
        sides = []
        for level in (pair, pair + 1):
            rows = [
                state[pl.ds((f * levels + level) * POINTS, POINTS), :] for f in range(FIELDS)
            ]
            rows.append(outer[pl.ds(level * 8 * FIELDS, 8 * FIELDS), :])
            rows.append(blank)
            sides.append(jnp.concatenate(rows, axis=0))
        values = jnp.concatenate(sides, axis=1)
        top = values.astype(jnp.bfloat16)
        rest = (values - top.astype(jnp.float32)).astype(jnp.bfloat16)
        change = (
            jnp.dot(high, top, preferred_element_type=jnp.float32)
            + jnp.dot(high, rest, preferred_element_type=jnp.float32)
            + jnp.dot(low, top, preferred_element_type=jnp.float32)
        )
        for place, level in enumerate((pair, pair + 1)):
            for f in range(FIELDS):
                at = pl.ds((f * levels + level) * POINTS, POINTS)
                part[at, :] = (
                    state[at, :]
                    + scale
                    * change[
                        f * POINTS : (f + 1) * POINTS, place * lanes : (place + 1) * lanes
                    ]
                )
    for level in range(levels):
        speed = part[pl.ds((3 * levels + level) * POINTS, POINTS), :]
        upper = part[pl.ds((4 * levels + level + 1) * POINTS, POINTS), :] if level < levels - 1 else 0.0
        lower = part[pl.ds((4 * levels + level - 1) * POINTS, POINTS), :] if level else 0.0
        value = speed - gravity_couple * (upper - lower)
        for j in range(NODES):
            base[j, level * NODES : (level + 1) * NODES, :] = value[NODES * j : NODES * (j + 1)]
    for extra, level in ((0, 0), (1, levels - 1)):
        value = part[pl.ds((4 * levels + level) * POINTS, POINTS), :]
        at = (levels + extra) * NODES
        for j in range(NODES):
            base[j, at : at + NODES, :] = value[NODES * j : NODES * (j + 1)]


def side_corrections(received, side, fluxes, fields, pieces):
    lanes = received.shape[1]
    sign = 1.0 if side == 0 else -1.0
    result = [[] for _ in fields]
    for piece in range(pieces):
        rows = []
        for g in range(FIELDS):
            block, at = side_rows(g, piece)
            rows.append(
                pltpu.roll(
                    received[block * ROWS : (block + 1) * ROWS, :], (lanes - at - side) % lanes, 1
                )
            )
        for place, f in enumerate(fields):
            result[place].append(rows[f] + sign * along(fluxes, 1, f, rows))
    return result


def spread(value, edge, masks, flip):
    lanes = value.shape[1]
    values = {
        point: pltpu.roll(value, (edge - 2 * place) % lanes, 1)
        for place, point in enumerate(RIM_POINTS)
    }
    return pick(values, masks, flip)


def add_first_side(partner, start, picked, send, base, metric):
    weight = 0.5 * lift_weight * step_size
    i = (NODES - 1) * partner_side(partner)
    for j, row in enumerate(picked):
        at = pl.ds(start * NODES + i, ROWS, stride=NODES)
        scale = weight * metric[pl.ds(NODES * j + i, 1), :]
        send[j, at, :] = base[j, at, :] + scale * row


def pack_kernel(half, from_other, neighbour_face, orientation, metric, *rest):
    sends, (send,) = rest[:NODES], rest[NODES:]
    me = lax.axis_index("vz")
    send[...] = half[...]
    rows, lanes = half.shape[1:]
    width = len(RIM_POINTS)
    face = partner_side(1)
    masks, flip = table_masks(
        neighbour_face[pl.ds(face, 1), :], orientation[pl.ds(face, 1), :], lanes
    )
    for start in chunks(rows // NODES):
        values = {
            point: from_other[pl.ds(start * width + place, ROWS, stride=width), :]
            for place, point in enumerate(RIM_POINTS)
        }
        add_first_side(1, start, pick(values, masks, flip), send, half, metric)
    for out, way in zip(sends, WAYS):
        out[...] = send[me ^ way]


def half_pack_kernel(
    base,
    from_down,
    from_up,
    neighbour_face,
    orientation,
    metric,
    fluxes,
    factored,
    half,
    send,
    column,
    mixed,
):
    rows, lanes = base.shape[1:]
    levels = rows // NODES - 2
    width = len(RIM_POINTS)
    weight = 0.5 * lift_weight * step_size
    send[:, 0:rows, :] = base[...]
    send[:, rows:, :] = jnp.zeros((NODES, send.shape[1] - rows, lanes), jnp.float32)
    column[...] = jnp.zeros_like(column)
    mixed[...] = jnp.zeros_like(mixed)
    lane = lax.broadcasted_iota(jnp.int32, (ROWS, lanes), 1)
    for side, (received, edge, j) in enumerate(
        ((from_down, 0, 0), (from_up, lanes - 1, NODES - 1))
    ):
        face = 2 + side
        masks, flip = table_masks(
            neighbour_face[face : face + 1, :], orientation[face : face + 1, :], lanes
        )
        speed, heat = side_corrections(received, side, fluxes, (3, 4), len(chunks(levels)))
        for start, value in zip(chunks(levels), heat):
            column[pl.ds(ROWS + start, ROWS), :] = value
        for start, value in zip(chunks(levels), speed):
            upper = column[pl.ds(ROWS + start + 1, ROWS), :]
            lower = column[pl.ds(ROWS + start - 1, ROWS), :]
            mixed[pl.ds(start, ROWS), :] = value - gravity_couple * (upper - lower)
        mixed[levels : levels + 1, :] = column[ROWS : ROWS + 1, :]
        mixed[levels + 1 : levels + 2, :] = column[ROWS + levels - 1 : ROWS + levels, :]
        for start in ends(levels + 2):
            picked = spread(mixed[start : start + ROWS, :], edge, masks, flip)
            for k, row in enumerate(picked):
                point = NODES * j + k
                at = pl.ds(start * NODES + k, ROWS, stride=NODES)
                scale = weight * metric[point : point + 1, :]
                send[j, at, :] += jnp.where(lane == edge, scale * row, 0.0)
    half[...] = send[:, 0:rows, :]


def finish_section_kernel(
    part,
    near,
    other_early,
    other_late,
    from_down,
    from_up,
    neighbour_face,
    orientation,
    metric,
    fluxes,
    out,
    done,
    final,
    semaphore,
):
    levels = part.shape[0] // (FIELDS * POINTS)
    lanes = part.shape[1]
    size = levels * POINTS
    weight = 0.5 * lift_weight * step_size
    scale = weight * metric[...]
    lane = lax.broadcasted_iota(jnp.int32, (ROWS, lanes), 1)
    tables = []
    edges = []
    for side, received in enumerate((from_down, from_up)):
        face = 2 + side
        tables.append(
            table_masks(
                neighbour_face[face : face + 1, :], orientation[face : face + 1, :], lanes
            )
        )
        edges.append(
            side_corrections(received, side, fluxes, LATE_FIELDS, len(chunks(levels)))
        )
    copy = pltpu.make_async_copy(final, out.at[1:3], semaphore)
    sources = ((near,), (other_early, other_late))
    for place, f in ((1, 1), (2, 2), (0, 0), (3, 4)):
        target = final.at[f - 1] if f in (1, 2) else done.at[min(f, 1)]
        target[...] = part[f * size : (f + 1) * size, :]
        for piece, start in enumerate(chunks(levels)):
            for j in range(NODES):
                for partner, source in enumerate(sources):
                    point = NODES * j + (NODES - 1) * partner_side(partner)
                    share = len(LATE_FIELDS) // len(source)
                    rows = source[place // share][
                        pl.ds(((place % share) * levels + start) * NODES + j, ROWS, stride=NODES),
                        :,
                    ]
                    at = pl.ds(start * POINTS + point, ROWS, stride=POINTS)
                    target[at, :] = (
                        part[pl.ds(f * size + start * POINTS + point, ROWS, stride=POINTS), :]
                        + weight * metric[pl.ds(point, 1), :] * rows
                    )
        for piece, start in enumerate(chunks(levels)):
            row_index = lax.broadcasted_iota(jnp.int32, (ROWS, lanes), 0)
            fresh = row_index >= (-start) % ROWS
            for side, (edge, j) in enumerate(((0, 0), (lanes - 1, NODES - 1))):
                picked = spread(edges[side][place][piece], edge, *tables[side])
                for k, row in enumerate(picked):
                    point = NODES * j + k
                    at = pl.ds(start * POINTS + point, ROWS, stride=POINTS)
                    target[at, :] += jnp.where(
                        (lane == edge) & fresh, scale[point : point + 1, :] * row, 0.0
                    )
        if f == 2:
            copy.start()
    copy.wait()


def factor_kernel(coupling, damping, inverse, near, far_two, far_three, ratio, next_two, next_three):
    levels = coupling.shape[1]
    blank = jnp.zeros(coupling.shape[2:], jnp.float32)
    far_ratio, far_second, near_ratio, near_second = (blank,) * 4
    far_before, near_before = blank, blank
    extra = damping[...]
    for level in range(levels):
        a, b, d, e = (coupling[entry, level] for entry in range(4))
        centre = a + b + d + e + extra
        reduced = -b + a * far_ratio
        pivot = centre + a * far_second - reduced * near_ratio
        scaled = 1.0 / pivot
        upper_ratio = (-d - reduced * near_second) * scaled
        second_ratio = -e * scaled
        far_here, near_here = a * scaled, reduced * scaled
        inverse[level] = scaled
        near[level] = near_here
        far_two[level] = far_here + near_here * near_before
        far_three[level] = near_here * far_before
        ratio[level] = upper_ratio
        if level:
            next_two[level - 1] = near_ratio * upper_ratio - near_second
            next_three[level - 1] = near_ratio * second_ratio
        far_before, near_before = far_here, near_here
        far_ratio, far_second = near_ratio, near_second
        near_ratio, near_second = upper_ratio, second_ratio
    next_two[levels - 1] = -near_second
    next_three[levels - 1] = blank


def solve_kernel(inverse, near, far_two, far_three, ratio, next_two, next_three, *rest):
    ways = NODES
    received, sends, (source, heat, speed) = rest[:ways], rest[ways : 2 * ways], rest[2 * ways :]
    levels = near.shape[0]
    here = levels // ways
    me = lax.axis_index("vz")
    for values, way in zip(received, WAYS):
        block = me ^ way
        source[pl.ds(block * here, here)] = values[0:here]
        heat[block] = values[here : here + 2]
    for block in range(ways - 1):
        last = block * here + here - 1
        source[last] = source[last] - gravity_couple * heat[block + 1, 0]
        source[last + 1] = source[last + 1] + gravity_couple * heat[block, 1]
    blank = jnp.zeros(near.shape[1:], jnp.float32)
    scaled = blank
    known = [blank, blank, blank]
    for level in range(levels):
        before, scaled = scaled, source[level] * inverse[level]
        value = scaled - near[level] * before - far_three[level] * known[-3]
        value = value + far_two[level] * known[-2]
        source[level] = value
        known = [*known[1:], value]
    speed[0] = blank
    speed[levels + 1] = blank
    known = [blank, blank, blank]
    above = blank
    for level in range(levels - 1, -1, -1):
        here_value = source[level]
        value = here_value - ratio[level] * above + next_three[level] * known[-3]
        value = value + next_two[level] * known[-2]
        speed[level + 1] = value
        above = here_value
        known = [*known[1:], value]
    for send, way in zip(sends, BACK_WAYS):
        send[...] = speed[pl.ds((me ^ way) * here, here + 2)]


def update_kernel(*refs):
    ways = NODES
    received, (done, earlier, out, speed, final, semaphores) = refs[:ways], refs[ways:]
    levels = done.shape[1] // POINTS
    me = lax.axis_index("vz")
    for values, way in zip(received, BACK_WAYS):
        speed[me ^ way] = values[...]
    lanes = done.shape[2]
    half = levels // 2
    low = lax.broadcasted_iota(jnp.int32, (ROWS, lanes), 0) < NODES
    copies = []
    for pair in range(half):
        lower = [speed[j, pair * ROWS : (pair + 1) * ROWS, :] for j in range(NODES)]
        upper = [speed[j, (pair + 1) * ROWS : (pair + 2) * ROWS, :] for j in range(NODES)]
        jump = [above - below for above, below in zip(upper, lower)]
        value = [jnp.where(low, above, below) for above, below in zip(upper, lower)]
        for h in range(2):
            a, b = 2 * h, 2 * h + 1
            for odd in range(2):
                at = pl.ds((2 * pair + odd) * POINTS + ROWS * h, ROWS)
                jumps = side_by_side(jump[a], jump[b], odd, low)
                final[0, at, :] = done[0, at, :] - density_couple * jumps
                final[1, at, :] = side_by_side(value[a], value[b], 1 - odd, low)
                final[2, at, :] = done[1, at, :] - theta_couple * jumps
        if pair in (half // 2 - 1, half - 1):
            first = 0 if pair < half - 1 else half // 2
            rows = pl.ds(first * 2 * POINTS, (pair + 1 - first) * 2 * POINTS)
            for place, f in enumerate((0, 3, 4)):
                copies.append(
                    pltpu.make_async_copy(
                        final.at[place, rows, :], out.at[f, rows, :], semaphores.at[len(copies)]
                    )
                )
                copies[-1].start()
    for copy in copies:
        copy.wait()


def side_by_side(first, second, upper, low):
    if upper:
        return jnp.where(low, pltpu.roll(first, NODES, 0), second)
    return jnp.where(low, first, pltpu.roll(second, NODES, 0))


VMEM = pl.BlockSpec(memory_space=pltpu.VMEM)
HBM = pl.BlockSpec(memory_space=pltpu.HBM)
ANY = pl.BlockSpec(memory_space=pl.ANY)


def call(kernel, outs, in_specs, scratch=(), cost=0, name=None):
    kinds = [x if hasattr(x, "dtype") else pltpu.VMEM(x, jnp.float32) for x in outs]
    return pl.pallas_call(
        kernel,
        out_shape=kinds,
        in_specs=in_specs,
        out_specs=[VMEM] * len(outs),
        scratch_shapes=list(scratch),
        compiler_params=pltpu.CompilerParams(vmem_limit_bytes=24 * 1024 * 1024),
        cost_estimate=pl.CostEstimate(flops=cost, bytes_accessed=cost, transcendentals=0),
        name=name,
    )


def per_device(
    prognostic, metric, first_flux, second_flux, neighbour_face, orientation, coupling, damping
):
    fields, levels = prognostic.shape[:2]
    lanes = prognostic.shape[-1]
    whole = (fields, levels * POINTS, lanes)
    metric = metric.reshape(POINTS, lanes)
    neighbour_face = neighbour_face.reshape(4, lanes)
    orientation = orientation.reshape(4, lanes)
    coupling = coupling.reshape(4, coupling.shape[1], NODES, lanes)
    damping = damping.reshape(NODES, lanes)
    tables, _ = operator_tables(lanes)

    def shifts(axis):
        size = lax.axis_size(axis)
        up = [(i, (i + 1) % size) for i in range(size)]
        return up, [(j, i) for i, j in up]

    def exchange(arrays, ways):
        size = lax.axis_size("vz")
        return [
            lax.ppermute(x, "vz", [(i, i ^ way) for i in range(size)]) if way else x
            for x, way in zip(arrays, ways)
        ]

    count = lax.axis_size("hy")
    near = [(i, i ^ 1) for i in range(count)]
    other = [(i, (i + 1 if i % 2 else i - 1) % count) for i in range(count)]
    second_up, second_down = shifts("hx")
    width = len(RIM_POINTS)
    message = (-(-((levels + 2) * width + 2) // ROWS) * ROWS, lanes)
    sides = (-(-fields * len(chunks(levels)) // 4) * ROWS, lanes)
    padded = levels + 2 * ROWS
    table = pltpu.VMEM((4, lanes), jnp.int32)
    inputs = (
        prognostic.reshape(whole),
        neighbour_face,
        orientation,
        metric,
        jnp.asarray(tables),
        first_flux,
        second_flux,
    )
    (
        to_other,
        state,
        neighbour_face,
        orientation,
        metric,
        tables,
        fluxes,
    ) = call(
        rim_kernel,
        [
            message,
            whole,
            table,
            table,
            (POINTS, lanes),
            tables.shape,
            (-(-2 * fields * fields // ROWS) * ROWS, lanes),
        ],
        [HBM] * len(inputs),
        [
            pltpu.VMEM((width, padded, lanes), jnp.float32),
            pltpu.VMEM((width, padded, lanes), jnp.float32),
            pltpu.SMEM((fields, fields), jnp.float32),
            pltpu.SMEM((fields, fields), jnp.float32),
            pltpu.SemaphoreType.DMA((6 + -(-levels // ROWS),)),
        ],
        cost=1000,
        name="rim",
    )(*(pltpu.with_memory_space_constraint(x, pltpu.HBM) for x in inputs))
    state = state.reshape(fields * levels * POINTS, lanes)
    from_other = lax.ppermute(to_other, "hy", other)
    from_near = lax.ppermute(state, "hy", near)
    (to_sides,) = call(edge_kernel, [sides], [VMEM], cost=1000, name="edge")(state)
    from_down = lax.ppermute(to_sides, "hx", second_up)
    from_up = from_down
    if lax.axis_size("hx") > 2:
        from_up = lax.ppermute(to_sides, "hx", second_down)

    column = (coupling.shape[1], NODES, lanes)
    factors = call(factor_kernel, [column] * 7, [VMEM] * 2, cost=4000000, name="factor")(
        coupling, damping
    )
    block = ((levels + 2) * NODES, lanes)
    part, base = call(
        element_kernel,
        [state.shape, (NODES,) + block],
        [VMEM] * 6,
        [
            pltpu.VMEM((levels * 8 * fields, lanes), jnp.float32),
            pltpu.VMEM((fields * POINTS, lanes), jnp.bfloat16),
            pltpu.VMEM((fields * POINTS, lanes), jnp.bfloat16),
        ],
        cost=4000000,
        name="element",
    )(
        state,
        neighbour_face,
        orientation,
        metric,
        fluxes,
        tables,
    )
    late = levels * NODES * len(LATE_FIELDS)
    base, near_late = call(
        near_kernel,
        [(NODES,) + block, (late, lanes)],
        [VMEM] * 6,
        [pltpu.VMEM((NODES, padded, lanes), jnp.float32), pltpu.VMEM(block, jnp.float32)],
        cost=1000,
        name="near",
    )(from_near, neighbour_face, orientation, fluxes, base, metric)
    count = -(-(levels + 2) // ROWS) * ROWS
    (half,) = call(
        half_pack_kernel,
        [(NODES,) + block],
        [VMEM] * 7 + [ANY],
        [
            pltpu.VMEM((NODES, count * NODES, lanes), jnp.float32),
            pltpu.VMEM((padded, lanes), jnp.float32),
            pltpu.VMEM((count, lanes), jnp.float32),
        ],
        cost=1000,
        name="half_pack",
    )(
        base,
        from_down,
        from_up,
        neighbour_face,
        orientation,
        metric,
        fluxes,
        factors[0],
    )
    sends = call(
        pack_kernel,
        [block] * NODES,
        [VMEM] * 5,
        [pltpu.VMEM((NODES,) + block, jnp.float32)],
        cost=1000,
        name="pack",
    )(half, from_other, neighbour_face, orientation, metric)
    received = exchange(sends, WAYS)

    other_face = call(
        functools.partial(face_kernel, 1),
        [(late // 2, lanes)] * 2,
        [VMEM] * 3 + [ANY],
        cost=1000,
        name="other_face",
    )(state, from_other, fluxes, sends[-1])
    other_face = [lax.ppermute(x, "hy", other) for x in other_face]

    cube = (levels + 2, NODES, lanes)
    speeds = call(
        solve_kernel,
        [cube] * NODES,
        [VMEM] * (7 + NODES),
        [
            pltpu.VMEM(column, jnp.float32),
            pltpu.VMEM((NODES, 2, NODES, lanes), jnp.float32),
            pltpu.VMEM((column[0] + 2,) + column[1:], jnp.float32),
        ],
        cost=1000,
        name="solve",
    )(*factors, *[x.reshape(cube) for x in received])
    returned = exchange([x.reshape(block) for x in speeds], BACK_WAYS)
    size = levels * POINTS
    limits = pltpu.CompilerParams(vmem_limit_bytes=24 * 1024 * 1024)
    earlier, done = pl.pallas_call(
        finish_section_kernel,
        out_shape=[
            jax.ShapeDtypeStruct(whole, jnp.float32),
            pltpu.VMEM((2, size, lanes), jnp.float32),
        ],
        in_specs=[VMEM] * 10,
        out_specs=[HBM, VMEM],
        scratch_shapes=[
            pltpu.VMEM((2, size, lanes), jnp.float32),
            pltpu.SemaphoreType.DMA,
        ],
        compiler_params=limits,
        cost_estimate=pl.CostEstimate(flops=4000000, bytes_accessed=4000000, transcendentals=0),
        name="finish",
    )(
        part, near_late, *other_face, from_down, from_up, neighbour_face, orientation, metric, fluxes
    )
    updated = pl.pallas_call(
        update_kernel,
        out_shape=jax.ShapeDtypeStruct(whole, jnp.float32),
        in_specs=[VMEM] * (1 + NODES) + [HBM],
        out_specs=HBM,
        input_output_aliases={1 + NODES: 0},
        scratch_shapes=[
            pltpu.VMEM((NODES,) + block, jnp.float32),
            pltpu.VMEM((3, size, lanes), jnp.float32),
            pltpu.SemaphoreType.DMA((6,)),
        ],
        compiler_params=limits,
        name="update",
    )(*returned, done, earlier)
    return updated.reshape(prognostic.shape)


def solution(mesh):
    placed = (
        P(None, "vz", None, None, "hy", "hx"),
        P(None, None, "hy", "hx"),
        P(),
        P(),
        P(None, "hy", "hx"),
        P(None, "hy", "hx"),
        P(None, None, "vz", None, "hy", "hx"),
        P("vz", None, "hy", "hx"),
    )
    return jax.shard_map(
        per_device,
        mesh=mesh,
        in_specs=placed,
        out_specs=P(None, "vz", None, None, "hy", "hx"),
        check_vma=False,
    )
```

profile of v0, /device:TPU:0, one launch (start us, length us, event | category | flops | bytes accessed | tf_op | source)
XLA Modules:
  0.0 25.9 jit_solution(1633142371586987732)
XLA Ops:
  0.0 0.0 copy-start
  0.0 1.4 %rim.1 = (f32[272,128]{1,0:T(8,128)S(1)}, f32[5,320,128]{2,1,0:T(8,128)S(1)}, s32[4,128]{1,0:T(4,128)S(1)}, s32[4,128]{1,0:T(4,128)S(1)}, f32[16,128]{1,0:T(8,12...) custom-call(f32[5,320,128]{2,1,0:T(8,128)} %bitcast.32, s32[4,128]{1,0:T(4,128)} %bitcast.34, s32[4,128]{1,0:T(4,128)} %bitcast.35, ...), custom_call_target="tpu_custom_call" | custom-call | flops 1000 | bytes 1000 | tf_op jit(solution)/shard_map/rim/pallas_call | solution.py:776
  1.4 0.5 %collective-permute-start = (f32[1600,128]{1,0:T(8,128)S(1)}, f32[1600,128]{1,0:T(8,128)S(1)}, u32[]{:S(2)}, u32[]{:S(2)}) collective-permute-start(f32[1600,128]{1,0:T(8,128)S(1)} %bitcast.18), channel_id=1, source_target_pairs={{0,4},{4,0},{8,12},{12,8},{1,5},{5,1},{9,13},{13,9},{2,6},{6,2},{1... | collective-permute-start | bytes 2457608 | tf_op jit(solution)/shard_map/ppermute | solution.py:800
  2.0 2.6 %collective-permute-start.2 = (f32[272,128]{1,0:T(8,128)S(1)}, f32[272,128]{1,0:T(8,128)S(1)}, u32[]{:S(2)}, u32[]{:S(2)}) collective-permute-start(f32[272,128]{1,0:T(8,128)S(1)} %get-tuple-element.50), channel_id=1, source_target_pairs={{0,12},{4,8},{8,4},{12,0},{1,13},{5,9},{9,5},{13,1},{2,14},{6,10},... | collective-permute-start | bytes 417800 | tf_op jit(solution)/shard_map/ppermute | solution.py:799
  4.6 0.3 %edge.1 = f32[32,128]{1,0:T(8,128)S(1)} custom-call(f32[1600,128]{1,0:T(8,128)S(1)} %bitcast.19), custom_call_target="tpu_custom_call" | custom-call | flops 1000 | bytes 1000 | tf_op jit(solution)/shard_map/edge/pallas_call | solution.py:801
  4.9 0.0 copy-start.1
  4.9 1.6 %collective-permute-start.1 = (f32[32,128]{1,0:T(8,128)S(1)}, f32[32,128]{1,0:T(8,128)S(1)}, u32[]{:S(2)}, u32[]{:S(2)}) collective-permute-start(f32[32,128]{1,0:T(8,128)S(1)} %edge.1), channel_id=1, source_target_pairs={{0,16},{16,0},{1,17},{17,1},{2,18},{18,2},{3,19},{19,3},{4,20},{20... | collective-permute-start | bytes 49160 | tf_op jit(solution)/shard_map/ppermute | solution.py:802
  6.5 0.0 copy-done
  6.5 0.0 copy-done.1
  6.5 0.7 %factor.1 = (f32[80,4,128]{2,1,0:T(4,128)S(1)}, f32[80,4,128]{2,1,0:T(4,128)S(1)}, f32[80,4,128]{2,1,0:T(4,128)S(1)}, f32[80,4,128]{2,1,0:T(4,128)S(1)}, f32[80,...) custom-call(f32[4,80,4,128]{3,2,1,0:T(4,128)S(1)} %bitcast.22, f32[4,128]{1,0:T(4,128)S(1)} %bitcast.28), custom_call_target="tpu_custom_call" | custom-call | flops 4000000 | bytes 4000000 | tf_op jit(solution)/shard_map/factor/pallas_call | solution.py:808
  7.2 0.8 %element.1 = (f32[1600,128]{1,0:T(8,128)S(1)}, f32[4,88,128]{2,1,0:T(8,128)S(1)}) custom-call(f32[1600,128]{1,0:T(8,128)S(1)} %bitcast.20, s32[4,128]{1,0:T(4,128)S(1)} %get-tuple-element.43.neighbour_face, s32[4,128]{1,0:T(4,128)S(1)} %get-tuple-element.44.orientation, f32[16,128]{1,0:T(8,128)S(1)} %get-tuple-element.46.metric, ...), custom_call_target="tpu_custom_call" | custom-call | flops 4000000 | bytes 4000000 | tf_op jit(solution)/shard_map/element/pallas_call | solution.py:812
  8.0 0.0 collective-permute-done.state
  8.0 0.3 %near.1 = (f32[4,88,128]{2,1,0:T(8,128)S(1)}, f32[320,128]{1,0:T(8,128)S(1)}) custom-call(f32[1600,128]{1,0:T(8,128)S(1)} %collective-permute-done.state, s32[4,128]{1,0:T(4,128)S(1)} %get-tuple-element.43.neighbour_face, s32[4,128]{1,0:T(4,128)S(1)} %get-tuple-element.44.orientation, f32[56,128]{1,0:T(8,128)S(1)} %get-tuple-element.45.fluxes, ...), custom_call_target="tpu_custom_call" | custom-call | flops 1000 | bytes 1000 | tf_op jit(solution)/shard_map/near/pallas_call | solution.py:832
  8.3 0.4 %collective-permute-done.1.from_down.from_up = f32[32,128]{1,0:T(8,128)S(1)} collective-permute-done((f32[32,128]{1,0:T(8,128)S(1)}, f32[32,128]{1,0:T(8,128)S(1)}, u32[]{:S(2)}, u32[]{:S(2)}) %collective-permute-start.1) | collective-permute-done | bytes 16416 | tf_op jit(solution)/shard_map/ppermute | solution.py:802
  8.7 0.2 half_pack.1.half
  9.0 0.0 collective-permute-done.2.from_other.received
  9.0 2.7 %collective-permute-start.3 = (f32[88,128]{1,0:T(8,128)S(1)}, f32[88,128]{1,0:T(8,128)S(1)}, u32[]{:S(2)}, u32[]{:S(2)}) collective-permute-start(f32[88,128]{1,0:T(8,128)S(1)} %get-tuple-element.51), channel_id=1, source_target_pairs={{0,2},{1,3},{2,0},{3,1},{4,6},{5,7},{6,4},{7,5},{8,10},{9,11},{10,... | collective-permute-start | bytes 135176 | tf_op jit(solution)/shard_map/ppermute | solution.py:746
  11.7 1.3 %collective-permute-start.4 = (f32[88,128]{1,0:T(8,128)S(1)}, f32[88,128]{1,0:T(8,128)S(1)}, u32[]{:S(2)}, u32[]{:S(2)}) collective-permute-start(f32[88,128]{1,0:T(8,128)S(1)} %get-tuple-element.52), channel_id=1, source_target_pairs={{0,3},{1,2},{2,1},{3,0},{4,7},{5,6},{6,5},{7,4},{8,11},{9,10},{10,... | collective-permute-start | bytes 135176 | tf_op jit(solution)/shard_map/ppermute | solution.py:746
  13.0 0.2 collective-permute-start.5
  13.3 0.3 other_face.1
  13.5 0.5 %collective-permute-start.9 = (f32[160,128]{1,0:T(8,128)S(1)}, f32[160,128]{1,0:T(8,128)S(1)}, u32[]{:S(2)}, u32[]{:S(2)}) collective-permute-start(f32[160,128]{1,0:T(8,128)S(1)} %get-tuple-element.61), channel_id=1, source_target_pairs={{0,12},{4,8},{8,4},{12,0},{1,13},{5,9},{9,5},{13,1},{2,14},{6,10},... | collective-permute-start | bytes 245768 | tf_op jit(solution)/shard_map/ppermute | solution.py:879
  14.0 1.3 %collective-permute-start.10 = (f32[160,128]{1,0:T(8,128)S(1)}, f32[160,128]{1,0:T(8,128)S(1)}, u32[]{:S(2)}, u32[]{:S(2)}) collective-permute-start(f32[160,128]{1,0:T(8,128)S(1)} %get-tuple-element.62), channel_id=1, source_target_pairs={{0,12},{4,8},{8,4},{12,0},{1,13},{5,9},{9,5},{13,1},{2,14},{6,10},... | collective-permute-start | bytes 245768 | tf_op jit(solution)/shard_map/ppermute | solution.py:879
  15.3 0.0 collective-permute-done.3
  15.3 2.2 %collective-permute-done.4 = f32[88,128]{1,0:T(8,128)S(1)} collective-permute-done((f32[88,128]{1,0:T(8,128)S(1)}, f32[88,128]{1,0:T(8,128)S(1)}, u32[]{:S(2)}, u32[]{:S(2)}) %collective-permute-start.4) | collective-permute-done | bytes 45088 | tf_op jit(solution)/shard_map/ppermute | solution.py:746
  17.6 0.0 collective-permute-done.5
  17.6 0.2 solve.1
  17.8 1.4 %collective-permute-start.7 = (f32[88,128]{1,0:T(8,128)S(1)}, f32[88,128]{1,0:T(8,128)S(1)}, u32[]{:S(2)}, u32[]{:S(2)}) collective-permute-start(f32[88,128]{1,0:T(8,128)S(1)} %bitcast.31), channel_id=1, source_target_pairs={{0,2},{1,3},{2,0},{3,1},{4,6},{5,7},{6,4},{7,5},{8,10},{9,11},{10,... | collective-permute-start | bytes 135176 | tf_op jit(solution)/shard_map/ppermute | solution.py:746
  19.2 1.1 %collective-permute-start.6 = (f32[88,128]{1,0:T(8,128)S(1)}, f32[88,128]{1,0:T(8,128)S(1)}, u32[]{:S(2)}, u32[]{:S(2)}) collective-permute-start(f32[88,128]{1,0:T(8,128)S(1)} %bitcast.30), channel_id=1, source_target_pairs={{0,3},{1,2},{2,1},{3,0},{4,7},{5,6},{6,5},{7,4},{8,11},{9,10},{10,... | collective-permute-start | bytes 135176 | tf_op jit(solution)/shard_map/ppermute | solution.py:746
  20.3 1.1 %collective-permute-start.8 = (f32[88,128]{1,0:T(8,128)S(1)}, f32[88,128]{1,0:T(8,128)S(1)}, u32[]{:S(2)}, u32[]{:S(2)}) collective-permute-start(f32[88,128]{1,0:T(8,128)S(1)} %bitcast.29), channel_id=1, source_target_pairs={{0,1},{1,0},{2,3},{3,2},{4,5},{5,4},{6,7},{7,6},{8,9},{9,8},{10,11... | collective-permute-start | bytes 135176 | tf_op jit(solution)/shard_map/ppermute | solution.py:746
  21.4 0.0 collective-permute-done.9.other_early
  21.4 0.0 collective-permute-done.10.other_late
  21.4 1.3 %finish.1 = (f32[5,320,128]{2,1,0:T(8,128)}, f32[2,320,128]{2,1,0:T(8,128)S(1)}) custom-call(f32[1600,128]{1,0:T(8,128)S(1)} %get-tuple-element.59.part, f32[320,128]{1,0:T(8,128)S(1)} %get-tuple-element.60.near, f32[160,128]{1,0:T(8,128)S(1)} %collective-permute-done.9.other_early, f32[160,128]{1,0:T(8,128)S(1)} %collective-permute-done.10.other_late, ...), custom_call_target="tpu_custom_call" | custom-call | flops 4000000 | bytes 4000000 | tf_op jit(solution)/shard_map/finish/pallas_call | solution.py:897
  22.7 0.6 %collective-permute-done.7.refs_1_ = f32[88,128]{1,0:T(8,128)S(1)} collective-permute-done((f32[88,128]{1,0:T(8,128)S(1)}, f32[88,128]{1,0:T(8,128)S(1)}, u32[]{:S(2)}, u32[]{:S(2)}) %collective-permute-start.7) | collective-permute-done | bytes 45088 | tf_op jit(solution)/shard_map/ppermute | solution.py:746
  23.3 1.7 %collective-permute-done.6.refs_0_ = f32[88,128]{1,0:T(8,128)S(1)} collective-permute-done((f32[88,128]{1,0:T(8,128)S(1)}, f32[88,128]{1,0:T(8,128)S(1)}, u32[]{:S(2)}, u32[]{:S(2)}) %collective-permute-start.6) | collective-permute-done | bytes 45088 | tf_op jit(solution)/shard_map/ppermute | solution.py:746
  25.0 0.0 collective-permute-done.8.refs_2_
  25.0 0.9 %update.1 = f32[5,320,128]{2,1,0:T(8,128)} custom-call(f32[88,128]{1,0:T(8,128)S(1)} %collective-permute-done.6.refs_0_, f32[88,128]{1,0:T(8,128)S(1)} %collective-permute-done.7.refs_1_, f32[88,128]{1,0:T(8,128)S(1)} %collective-permute-done.8.refs_2_, f32[88,128]{1,0:T(8,128)S(1)} %bitcast.24, ...), custom_call_target="tpu_custom_call", output_to_operand_aliasing={{}: (5, {})} | custom-call | tf_op jit(solution)/shard_map/update/pallas_call | solution.py:915
  (1 shorter events, 0.0 us)
Async XLA Ops:
  0.0 6.5 %copy-start = (f32[4,80,1,4,1,128]{5,4,3,2,1,0:T(1,128)S(1)}, f32[4,80,1,4,1,128]{5,4,3,2,1,0:T(1,128)}, u32[]{:S(2)}) copy-start(f32[4,80,1,4,1,128]{5,4,3,2,1,0:T(1,128)} %param.15) | copy-start | bytes 1966084
  1.4 6.6 %collective-permute-start = (f32[1600,128]{1,0:T(8,128)S(1)}, f32[1600,128]{1,0:T(8,128)S(1)}, u32[]{:S(2)}, u32[]{:S(2)}) collective-permute-start(f32[1600,128]{1,0:T(8,128)S(1)} %bitcast.18), channel_id=1, source_target_pairs={{0,4},{4,0},{8,12},{12,8},{1,5},{5,1},{9,13},{13,9},{2,6},{6,2},{1... | collective-permute-start | bytes 2457608 | tf_op jit(solution)/shard_map/ppermute | solution.py:800
  2.0 7.0 %collective-permute-start.2 = (f32[272,128]{1,0:T(8,128)S(1)}, f32[272,128]{1,0:T(8,128)S(1)}, u32[]{:S(2)}, u32[]{:S(2)}) collective-permute-start(f32[272,128]{1,0:T(8,128)S(1)} %get-tuple-element.50), channel_id=1, source_target_pairs={{0,12},{4,8},{8,4},{12,0},{1,13},{5,9},{9,5},{13,1},{2,14},{6,10},... | collective-permute-start | bytes 417800 | tf_op jit(solution)/shard_map/ppermute | solution.py:799
  4.9 1.6 %copy-start.1 = (f32[1,4,1,128]{3,2,1,0:T(1,128)S(1)}, f32[1,4,1,128]{3,2,1,0:T(1,128)}, u32[]{:S(2)}) copy-start(f32[1,4,1,128]{3,2,1,0:T(1,128)} %param.16) | copy-start | bytes 6148
  4.9 3.8 %collective-permute-start.1 = (f32[32,128]{1,0:T(8,128)S(1)}, f32[32,128]{1,0:T(8,128)S(1)}, u32[]{:S(2)}, u32[]{:S(2)}) collective-permute-start(f32[32,128]{1,0:T(8,128)S(1)} %edge.1), channel_id=1, source_target_pairs={{0,16},{16,0},{1,17},{17,1},{2,18},{18,2},{3,19},{19,3},{4,20},{20... | collective-permute-start | bytes 49160 | tf_op jit(solution)/shard_map/ppermute | solution.py:802
  9.0 6.3 %collective-permute-start.3 = (f32[88,128]{1,0:T(8,128)S(1)}, f32[88,128]{1,0:T(8,128)S(1)}, u32[]{:S(2)}, u32[]{:S(2)}) collective-permute-start(f32[88,128]{1,0:T(8,128)S(1)} %get-tuple-element.51), channel_id=1, source_target_pairs={{0,2},{1,3},{2,0},{3,1},{4,6},{5,7},{6,4},{7,5},{8,10},{9,11},{10,... | collective-permute-start | bytes 135176 | tf_op jit(solution)/shard_map/ppermute | solution.py:746
  11.7 5.9 %collective-permute-start.4 = (f32[88,128]{1,0:T(8,128)S(1)}, f32[88,128]{1,0:T(8,128)S(1)}, u32[]{:S(2)}, u32[]{:S(2)}) collective-permute-start(f32[88,128]{1,0:T(8,128)S(1)} %get-tuple-element.52), channel_id=1, source_target_pairs={{0,3},{1,2},{2,1},{3,0},{4,7},{5,6},{6,5},{7,4},{8,11},{9,10},{10,... | collective-permute-start | bytes 135176 | tf_op jit(solution)/shard_map/ppermute | solution.py:746
  13.0 4.5 %collective-permute-start.5 = (f32[88,128]{1,0:T(8,128)S(1)}, f32[88,128]{1,0:T(8,128)S(1)}, u32[]{:S(2)}, u32[]{:S(2)}) collective-permute-start(f32[88,128]{1,0:T(8,128)S(1)} %get-tuple-element.53), channel_id=1, source_target_pairs={{0,1},{1,0},{2,3},{3,2},{4,5},{5,4},{6,7},{7,6},{8,9},{9,8},{10,11... | collective-permute-start | bytes 135176 | tf_op jit(solution)/shard_map/ppermute | solution.py:746
  13.5 7.8 %collective-permute-start.9 = (f32[160,128]{1,0:T(8,128)S(1)}, f32[160,128]{1,0:T(8,128)S(1)}, u32[]{:S(2)}, u32[]{:S(2)}) collective-permute-start(f32[160,128]{1,0:T(8,128)S(1)} %get-tuple-element.61), channel_id=1, source_target_pairs={{0,12},{4,8},{8,4},{12,0},{1,13},{5,9},{9,5},{13,1},{2,14},{6,10},... | collective-permute-start | bytes 245768 | tf_op jit(solution)/shard_map/ppermute | solution.py:879
  14.0 7.4 %collective-permute-start.10 = (f32[160,128]{1,0:T(8,128)S(1)}, f32[160,128]{1,0:T(8,128)S(1)}, u32[]{:S(2)}, u32[]{:S(2)}) collective-permute-start(f32[160,128]{1,0:T(8,128)S(1)} %get-tuple-element.62), channel_id=1, source_target_pairs={{0,12},{4,8},{8,4},{12,0},{1,13},{5,9},{9,5},{13,1},{2,14},{6,10},... | collective-permute-start | bytes 245768 | tf_op jit(solution)/shard_map/ppermute | solution.py:879
  17.8 5.5 %collective-permute-start.7 = (f32[88,128]{1,0:T(8,128)S(1)}, f32[88,128]{1,0:T(8,128)S(1)}, u32[]{:S(2)}, u32[]{:S(2)}) collective-permute-start(f32[88,128]{1,0:T(8,128)S(1)} %bitcast.31), channel_id=1, source_target_pairs={{0,2},{1,3},{2,0},{3,1},{4,6},{5,7},{6,4},{7,5},{8,10},{9,11},{10,... | collective-permute-start | bytes 135176 | tf_op jit(solution)/shard_map/ppermute | solution.py:746
  19.2 5.8 %collective-permute-start.6 = (f32[88,128]{1,0:T(8,128)S(1)}, f32[88,128]{1,0:T(8,128)S(1)}, u32[]{:S(2)}, u32[]{:S(2)}) collective-permute-start(f32[88,128]{1,0:T(8,128)S(1)} %bitcast.30), channel_id=1, source_target_pairs={{0,3},{1,2},{2,1},{3,0},{4,7},{5,6},{6,5},{7,4},{8,11},{9,10},{10,... | collective-permute-start | bytes 135176 | tf_op jit(solution)/shard_map/ppermute | solution.py:746
  20.3 4.7 %collective-permute-start.8 = (f32[88,128]{1,0:T(8,128)S(1)}, f32[88,128]{1,0:T(8,128)S(1)}, u32[]{:S(2)}, u32[]{:S(2)}) collective-permute-start(f32[88,128]{1,0:T(8,128)S(1)} %bitcast.29), channel_id=1, source_target_pairs={{0,1},{1,0},{2,3},{3,2},{4,5},{5,4},{6,7},{7,6},{8,9},{9,8},{10,11... | collective-permute-start | bytes 135176 | tf_op jit(solution)/shard_map/ppermute | solution.py:746
where the time goes:
time: 26.1 us; the launch traced here: 25.9 us
  starting transfers between devices  14.3 us (55%)
  Pallas kernels  6.55 us (25%)
  waiting for transfers between devices  4.97 us (19%)
    ppermute x6, starting transfers between devices, exchange(): lax.ppermute(x, 'vz', [(i, i ^ way) for i in range(size)])  7.79 us
    ppermute x6, waiting for transfers between devices, exchange(): lax.ppermute(x, 'vz', [(i, i ^ way) for i in range(size)])  4.58 us
    ppermute x1, starting transfers between devices, per_device(): from_other = lax.ppermute(to_other, 'hy', other)  2.64 us
    ppermute x2, starting transfers between devices, per_device(): other_face = [lax.ppermute(x, 'hy', other) for x in other_face]  1.81 us
    ppermute x1, starting transfers between devices, per_device(): from_down = lax.ppermute(to_sides, 'hx', second_up)  1.56 us
    pallas_call x1, Pallas kernels, per_device(): call(rim_kernel, [message, whole, table, table, (POINTS, lanes), tables.s...  1.44 us
    pallas_call x1, Pallas kernels, per_device(): pl.pallas_call(finish_section_kernel, out_shape=[jax.ShapeDtypeStruct(who...  1.33 us
    pallas_call x1, Pallas kernels, per_device(): pl.pallas_call(update_kernel, out_shape=jax.ShapeDtypeStruct(whole, jnp.f...  0.88 us
  transfers between devices with their start and end apart: 11, of which 4 were waited for; matrix products, arithmetic and copies ran while one was open for 0% of the time, Pallas kernels for 16%

commit v1 on v0

--- a/solution.py
+++ b/solution.py
@@ -21,7 +21,8 @@
 RIM_POINTS = tuple(sorted(set(sum(FACE_POINTS, ()))))
 ROWS = 8
 LATE_FIELDS = (0, 1, 2, 4)
-WAYS = (2, 3, 1, 0)
+WAYS = (3, 3, 2, 1, 0)
+FORWARD_ROOM = (0, 2, 2, 2, 0)
 BACK_WAYS = (3, 2, 1, 0)
 
 
@@ -454,7 +455,7 @@
 
 
 def pack_kernel(half, from_other, neighbour_face, orientation, metric, *rest):
-    sends, (send,) = rest[:NODES], rest[NODES:]
+    sends, (send,) = rest[: NODES + 1], rest[NODES + 1 :]
     me = lax.axis_index("vz")
     send[...] = half[...]
     rows, lanes = half.shape[1:]
@@ -470,7 +471,9 @@
         }
         add_first_side(1, start, pick(values, masks, flip), send, half, metric)
     for out, way in zip(sends, WAYS):
-        out[...] = send[me ^ way]
+        out[0:rows, :] = send[me ^ way]
+        if out.shape[0] > rows:
+            out[rows:, :] = jnp.zeros((out.shape[0] - rows, lanes), jnp.float32)
 
 
 def half_pack_kernel(
@@ -623,11 +626,13 @@
 
 def solve_kernel(inverse, near, far_two, far_three, ratio, next_two, next_three, *rest):
     ways = NODES
-    received, sends, (source, heat, speed) = rest[:ways], rest[ways : 2 * ways], rest[2 * ways :]
+    fallen, middle, risen, beside, own = rest[: ways + 1]
+    sends, (source, heat, speed) = rest[ways + 1 : 2 * ways + 1], rest[2 * ways + 1 :]
     levels = near.shape[0]
     here = levels // ways
     me = lax.axis_index("vz")
-    for values, way in zip(received, WAYS):
+    far = jnp.where(me < ways // 2, fallen[0 : here + 2], risen[0 : here + 2])
+    for values, way in ((far, 3), (middle, 2), (beside, 1), (own, 0)):
         block = me ^ way
         source[pl.ds(block * here, here)] = values[0:here]
         heat[block] = values[here : here + 2]
@@ -861,13 +866,19 @@
     )
     sends = call(
         pack_kernel,
-        [block] * NODES,
+        [((levels + 2 + more) * NODES, lanes) for more in FORWARD_ROOM],
         [VMEM] * 5,
         [pltpu.VMEM((NODES,) + block, jnp.float32)],
         cost=1000,
         name="pack",
     )(half, from_other, neighbour_face, orientation, metric)
-    received = exchange(sends, WAYS)
+    size = lax.axis_size("vz")
+    falls = [(i, i ^ 3) for i in range(size) if i > i ^ 3]
+    rises = [(j, i) for i, j in falls]
+    fallen = lax.ppermute(sends[0], "vz", falls)
+    risen = lax.ppermute(sends[1], "vz", rises)
+    middle, beside, own = exchange(sends[2:], WAYS[2:])
+    received = [fallen, middle, risen, beside, own]
 
     other_face = call(
         functools.partial(face_kernel, 1),
@@ -882,7 +893,7 @@
     speeds = call(
         solve_kernel,
         [cube] * NODES,
-        [VMEM] * (7 + NODES),
+        [VMEM] * (7 + 1 + NODES),
         [
             pltpu.VMEM(column, jnp.float32),
             pltpu.VMEM((NODES, 2, NODES, lanes), jnp.float32),
@@ -890,7 +901,7 @@
         ],
         cost=1000,
         name="solve",
-    )(*factors, *[x.reshape(cube) for x in received])
+    )(*factors, *[x.reshape(-1, NODES, lanes) for x in received])
     returned = exchange([x.reshape(block) for x in speeds], BACK_WAYS)
     size = levels * POINTS
     limits = pltpu.CompilerParams(vmem_limit_bytes=24 * 1024 * 1024)

time: 26.1 us -> 29.1 us (1.11)
  starting transfers between devices: 14.3 us -> 17.9 us
  waiting for transfers between devices: 4.97 us -> 4.4 us
    ppermute x0 -> x2, starting transfers between devices: none -> 4 us  [the longest x1 2.7 us: per_device(): risen = lax.ppermute(sends[1], 'vz', rises)]
    ppermute x6 -> x5, waiting for transfers between devices: 4.58 us -> 4 us  [exchange(): lax.ppermute(x, 'vz', [(i, i ^ way) for i in range(size)])]
    ppermute x6 -> x5, starting transfers between devices: 7.79 us -> 7.34 us  [exchange(): lax.ppermute(x, 'vz', [(i, i ^ way) for i in range(size)])]
  transfers between devices with their start and end apart: 11 -> 12, of which waited for: 4 -> 5; matrix products, arithmetic and copies ran while one was open for 0% -> 0% of each run, Pallas kernels for 16% -> 15%
where the time goes in v1:
time: 29.1 us; the launch traced here: 28.9 us
  starting transfers between devices  17.9 us (62%)
  Pallas kernels  6.56 us (23%)
  waiting for transfers between devices  4.4 us (15%)
    ppermute x5, starting transfers between devices, exchange(): lax.ppermute(x, 'vz', [(i, i ^ way) for i in range(size)])  7.34 us
    ppermute x5, waiting for transfers between devices, exchange(): lax.ppermute(x, 'vz', [(i, i ^ way) for i in range(size)])  4 us
    ppermute x1, starting transfers between devices, per_device(): risen = lax.ppermute(sends[1], 'vz', rises)  2.7 us
    ppermute x1, starting transfers between devices, per_device(): from_other = lax.ppermute(to_other, 'hy', other)  2.64 us
    ppermute x2, starting transfers between devices, per_device(): other_face = [lax.ppermute(x, 'hy', other) for x in other_face]  1.81 us
    ppermute x1, starting transfers between devices, per_device(): from_down = lax.ppermute(to_sides, 'hx', second_up)  1.56 us
    pallas_call x1, Pallas kernels, per_device(): call(rim_kernel, [message, whole, table, table, (POINTS, lanes), tables.s...  1.44 us
    pallas_call x1, Pallas kernels, per_device(): pl.pallas_call(finish_section_kernel, out_shape=[jax.ShapeDtypeStruct(who...  1.33 us
  transfers between devices with their start and end apart: 12, of which 5 were waited for; matrix products, arithmetic and copies ran while one was open for 0% of the time, Pallas kernels for 15%

profile of v1, /device:TPU:0, one launch (start us, length us, event | category | flops | bytes accessed | tf_op | source)
XLA Modules:
  0.0 28.9 jit_solution(9100308330006594974)
XLA Ops:
  0.0 0.0 copy-start
  0.0 1.4 %rim.1 = (f32[272,128]{1,0:T(8,128)S(1)}, f32[5,320,128]{2,1,0:T(8,128)S(1)}, s32[4,128]{1,0:T(4,128)S(1)}, s32[4,128]{1,0:T(4,128)S(1)}, f32[16,128]{1,0:T(8,12...) custom-call(f32[5,320,128]{2,1,0:T(8,128)} %bitcast.34, s32[4,128]{1,0:T(4,128)} %bitcast.36, s32[4,128]{1,0:T(4,128)} %bitcast.37, ...), custom_call_target="tpu_custom_call" | custom-call | flops 1000 | bytes 1000 | tf_op jit(solution)/shard_map/rim/pallas_call | solution.py:781
  1.4 0.5 %collective-permute-start = (f32[1600,128]{1,0:T(8,128)S(1)}, f32[1600,128]{1,0:T(8,128)S(1)}, u32[]{:S(2)}, u32[]{:S(2)}) collective-permute-start(f32[1600,128]{1,0:T(8,128)S(1)} %bitcast.19), channel_id=1, source_target_pairs={{0,4},{4,0},{8,12},{12,8},{1,5},{5,1},{9,13},{13,9},{2,6},{6,2},{1... | collective-permute-start | bytes 2457608 | tf_op jit(solution)/shard_map/ppermute | solution.py:805
  2.0 2.6 %collective-permute-start.2 = (f32[272,128]{1,0:T(8,128)S(1)}, f32[272,128]{1,0:T(8,128)S(1)}, u32[]{:S(2)}, u32[]{:S(2)}) collective-permute-start(f32[272,128]{1,0:T(8,128)S(1)} %get-tuple-element.51), channel_id=1, source_target_pairs={{0,12},{4,8},{8,4},{12,0},{1,13},{5,9},{9,5},{13,1},{2,14},{6,10},... | collective-permute-start | bytes 417800 | tf_op jit(solution)/shard_map/ppermute | solution.py:804
  4.6 0.3 edge.1
  4.9 0.0 copy-start.1
  4.9 1.6 %collective-permute-start.1 = (f32[32,128]{1,0:T(8,128)S(1)}, f32[32,128]{1,0:T(8,128)S(1)}, u32[]{:S(2)}, u32[]{:S(2)}) collective-permute-start(f32[32,128]{1,0:T(8,128)S(1)} %edge.1), channel_id=1, source_target_pairs={{0,16},{16,0},{1,17},{17,1},{2,18},{18,2},{3,19},{19,3},{4,20},{20... | collective-permute-start | bytes 49160 | tf_op jit(solution)/shard_map/ppermute | solution.py:807
  6.5 0.0 copy-done
  6.5 0.0 copy-done.1
  6.5 0.7 %factor.1 = (f32[80,4,128]{2,1,0:T(4,128)S(1)}, f32[80,4,128]{2,1,0:T(4,128)S(1)}, f32[80,4,128]{2,1,0:T(4,128)S(1)}, f32[80,4,128]{2,1,0:T(4,128)S(1)}, f32[80,...) custom-call(f32[4,80,4,128]{3,2,1,0:T(4,128)S(1)} %bitcast.23, f32[4,128]{1,0:T(4,128)S(1)} %bitcast.30), custom_call_target="tpu_custom_call" | custom-call | flops 4000000 | bytes 4000000 | tf_op jit(solution)/shard_map/factor/pallas_call | solution.py:813
  7.2 0.8 %element.1 = (f32[1600,128]{1,0:T(8,128)S(1)}, f32[4,88,128]{2,1,0:T(8,128)S(1)}) custom-call(f32[1600,128]{1,0:T(8,128)S(1)} %bitcast.21, s32[4,128]{1,0:T(4,128)S(1)} %get-tuple-element.44.neighbour_face, s32[4,128]{1,0:T(4,128)S(1)} %get-tuple-element.45.orientation, f32[16,128]{1,0:T(8,128)S(1)} %get-tuple-element.47.metric, ...), custom_call_target="tpu_custom_call" | custom-call | flops 4000000 | bytes 4000000 | tf_op jit(solution)/shard_map/element/pallas_call | solution.py:817
  8.0 0.0 collective-permute-done.state
  8.0 0.3 %near.1 = (f32[4,88,128]{2,1,0:T(8,128)S(1)}, f32[320,128]{1,0:T(8,128)S(1)}) custom-call(f32[1600,128]{1,0:T(8,128)S(1)} %collective-permute-done.state, s32[4,128]{1,0:T(4,128)S(1)} %get-tuple-element.44.neighbour_face, s32[4,128]{1,0:T(4,128)S(1)} %get-tuple-element.45.orientation, f32[56,128]{1,0:T(8,128)S(1)} %get-tuple-element.46.fluxes, ...), custom_call_target="tpu_custom_call" | custom-call | flops 1000 | bytes 1000 | tf_op jit(solution)/shard_map/near/pallas_call | solution.py:837
  8.3 0.4 %collective-permute-done.1.from_down.from_up = f32[32,128]{1,0:T(8,128)S(1)} collective-permute-done((f32[32,128]{1,0:T(8,128)S(1)}, f32[32,128]{1,0:T(8,128)S(1)}, u32[]{:S(2)}, u32[]{:S(2)}) %collective-permute-start.1) | collective-permute-done | bytes 16416 | tf_op jit(solution)/shard_map/ppermute | solution.py:807
  8.7 0.2 half_pack.1.half
  9.0 0.0 collective-permute-done.2.from_other.received
  9.0 0.1 pack.1
  9.0 1.3 %collective-permute-start.3 = (f32[88,128]{1,0:T(8,128)S(1)}, f32[88,128]{1,0:T(8,128)S(1)}, u32[]{:S(2)}, u32[]{:S(2)}) collective-permute-start(f32[88,128]{1,0:T(8,128)S(1)} %get-tuple-element.52), channel_id=1, source_target_pairs={{2,1},{3,0},{6,5},{7,4},{10,9},{11,8},{14,13},{15,12},{18,17},{19,... | collective-permute-start | bytes 135176 | tf_op jit(solution)/shard_map/ppermute | solution.py:878
  10.3 3.7 %collective-permute-start.4 = (f32[96,128]{1,0:T(8,128)S(1)}, f32[96,128]{1,0:T(8,128)S(1)}, u32[]{:S(2)}, u32[]{:S(2)}) collective-permute-start(f32[96,128]{1,0:T(8,128)S(1)} %get-tuple-element.53), channel_id=1, source_target_pairs={{0,2},{1,3},{2,0},{3,1},{4,6},{5,7},{6,4},{7,5},{8,10},{9,11},{10,... | collective-permute-start | bytes 147464 | tf_op jit(solution)/shard_map/ppermute | solution.py:751
  14.0 2.7 %collective-permute-start.5 = (f32[96,128]{1,0:T(8,128)S(1)}, f32[96,128]{1,0:T(8,128)S(1)}, u32[]{:S(2)}, u32[]{:S(2)}) collective-permute-start(f32[96,128]{1,0:T(8,128)S(1)} %get-tuple-element.54), channel_id=1, source_target_pairs={{1,2},{0,3},{5,6},{4,7},{9,10},{8,11},{13,14},{12,15},{17,18},{16,... | collective-permute-start | bytes 147464 | tf_op jit(solution)/shard_map/ppermute | solution.py:879
  16.8 0.1 collective-permute-start.6
  16.8 0.3 other_face.1
  17.1 0.5 %collective-permute-start.10 = (f32[160,128]{1,0:T(8,128)S(1)}, f32[160,128]{1,0:T(8,128)S(1)}, u32[]{:S(2)}, u32[]{:S(2)}) collective-permute-start(f32[160,128]{1,0:T(8,128)S(1)} %get-tuple-element.63), channel_id=1, source_target_pairs={{0,12},{4,8},{8,4},{12,0},{1,13},{5,9},{9,5},{13,1},{2,14},{6,10},... | collective-permute-start | bytes 245768 | tf_op jit(solution)/shard_map/ppermute | solution.py:890
  17.6 0.0 collective-permute-done.3
  17.6 1.3 %collective-permute-start.11 = (f32[160,128]{1,0:T(8,128)S(1)}, f32[160,128]{1,0:T(8,128)S(1)}, u32[]{:S(2)}, u32[]{:S(2)}) collective-permute-start(f32[160,128]{1,0:T(8,128)S(1)} %get-tuple-element.64), channel_id=1, source_target_pairs={{0,12},{4,8},{8,4},{12,0},{1,13},{5,9},{9,5},{13,1},{2,14},{6,10},... | collective-permute-start | bytes 245768 | tf_op jit(solution)/shard_map/ppermute | solution.py:890
  18.9 0.0 collective-permute-done.4
  18.9 0.0 collective-permute-done.5
  18.9 2.0 %collective-permute-done.6 = f32[96,128]{1,0:T(8,128)S(1)} collective-permute-done((f32[96,128]{1,0:T(8,128)S(1)}, f32[96,128]{1,0:T(8,128)S(1)}, u32[]{:S(2)}, u32[]{:S(2)}) %collective-permute-start.6) | collective-permute-done | bytes 49184 | tf_op jit(solution)/shard_map/ppermute | solution.py:751
  20.9 0.2 solve.1
  21.2 0.1 collective-permute-start.8
  21.2 2.8 %collective-permute-start.7 = (f32[88,128]{1,0:T(8,128)S(1)}, f32[88,128]{1,0:T(8,128)S(1)}, u32[]{:S(2)}, u32[]{:S(2)}) collective-permute-start(f32[88,128]{1,0:T(8,128)S(1)} %bitcast.32), channel_id=1, source_target_pairs={{0,3},{1,2},{2,1},{3,0},{4,7},{5,6},{6,5},{7,4},{8,11},{9,10},{10,... | collective-permute-start | bytes 135176 | tf_op jit(solution)/shard_map/ppermute | solution.py:751
  24.0 0.7 %collective-permute-start.9 = (f32[88,128]{1,0:T(8,128)S(1)}, f32[88,128]{1,0:T(8,128)S(1)}, u32[]{:S(2)}, u32[]{:S(2)}) collective-permute-start(f32[88,128]{1,0:T(8,128)S(1)} %bitcast.31), channel_id=1, source_target_pairs={{0,1},{1,0},{2,3},{3,2},{4,5},{5,4},{6,7},{7,6},{8,9},{9,8},{10,11... | collective-permute-start | bytes 135176 | tf_op jit(solution)/shard_map/ppermute | solution.py:751
  24.7 0.0 collective-permute-done.10.other_early
  24.7 0.0 collective-permute-done.11.other_late
  24.7 1.3 %finish.1 = (f32[5,320,128]{2,1,0:T(8,128)}, f32[2,320,128]{2,1,0:T(8,128)S(1)}) custom-call(f32[1600,128]{1,0:T(8,128)S(1)} %get-tuple-element.61.part, f32[320,128]{1,0:T(8,128)S(1)} %get-tuple-element.62.near, f32[160,128]{1,0:T(8,128)S(1)} %collective-permute-done.10.other_early, f32[160,128]{1,0:T(8,128)S(1)} %collective-permute-done.11.other_late, ...), custom_call_target="tpu_custom_call" | custom-call | flops 4000000 | bytes 4000000 | tf_op jit(solution)/shard_map/finish/pallas_call | solution.py:908
  26.1 0.5 %collective-permute-done.8.refs_1_ = f32[88,128]{1,0:T(8,128)S(1)} collective-permute-done((f32[88,128]{1,0:T(8,128)S(1)}, f32[88,128]{1,0:T(8,128)S(1)}, u32[]{:S(2)}, u32[]{:S(2)}) %collective-permute-start.8) | collective-permute-done | bytes 45088 | tf_op jit(solution)/shard_map/ppermute | solution.py:751
  26.5 0.7 %collective-permute-done.7.refs_0_ = f32[88,128]{1,0:T(8,128)S(1)} collective-permute-done((f32[88,128]{1,0:T(8,128)S(1)}, f32[88,128]{1,0:T(8,128)S(1)}, u32[]{:S(2)}, u32[]{:S(2)}) %collective-permute-start.7) | collective-permute-done | bytes 45088 | tf_op jit(solution)/shard_map/ppermute | solution.py:751
  27.3 0.8 %collective-permute-done.9.refs_2_ = f32[88,128]{1,0:T(8,128)S(1)} collective-permute-done((f32[88,128]{1,0:T(8,128)S(1)}, f32[88,128]{1,0:T(8,128)S(1)}, u32[]{:S(2)}, u32[]{:S(2)}) %collective-permute-start.9) | collective-permute-done | bytes 45088 | tf_op jit(solution)/shard_map/ppermute | solution.py:751
  28.1 0.9 %update.1 = f32[5,320,128]{2,1,0:T(8,128)} custom-call(f32[88,128]{1,0:T(8,128)S(1)} %collective-permute-done.7.refs_0_, f32[88,128]{1,0:T(8,128)S(1)} %collective-permute-done.8.refs_1_, f32[88,128]{1,0:T(8,128)S(1)} %collective-permute-done.9.refs_2_, f32[88,128]{1,0:T(8,128)S(1)} %bitcast.29, ...), custom_call_target="tpu_custom_call", output_to_operand_aliasing={{}: (5, {})} | custom-call | tf_op jit(solution)/shard_map/update/pallas_call | solution.py:926
Async XLA Ops:
  0.0 6.5 %copy-start = (f32[4,80,1,4,1,128]{5,4,3,2,1,0:T(1,128)S(1)}, f32[4,80,1,4,1,128]{5,4,3,2,1,0:T(1,128)}, u32[]{:S(2)}) copy-start(f32[4,80,1,4,1,128]{5,4,3,2,1,0:T(1,128)} %param.15) | copy-start | bytes 1966084
  1.4 6.6 %collective-permute-start = (f32[1600,128]{1,0:T(8,128)S(1)}, f32[1600,128]{1,0:T(8,128)S(1)}, u32[]{:S(2)}, u32[]{:S(2)}) collective-permute-start(f32[1600,128]{1,0:T(8,128)S(1)} %bitcast.19), channel_id=1, source_target_pairs={{0,4},{4,0},{8,12},{12,8},{1,5},{5,1},{9,13},{13,9},{2,6},{6,2},{1... | collective-permute-start | bytes 2457608 | tf_op jit(solution)/shard_map/ppermute | solution.py:805
  2.0 7.0 %collective-permute-start.2 = (f32[272,128]{1,0:T(8,128)S(1)}, f32[272,128]{1,0:T(8,128)S(1)}, u32[]{:S(2)}, u32[]{:S(2)}) collective-permute-start(f32[272,128]{1,0:T(8,128)S(1)} %get-tuple-element.51), channel_id=1, source_target_pairs={{0,12},{4,8},{8,4},{12,0},{1,13},{5,9},{9,5},{13,1},{2,14},{6,10},... | collective-permute-start | bytes 417800 | tf_op jit(solution)/shard_map/ppermute | solution.py:804
  4.9 1.6 %copy-start.1 = (f32[1,4,1,128]{3,2,1,0:T(1,128)S(1)}, f32[1,4,1,128]{3,2,1,0:T(1,128)}, u32[]{:S(2)}) copy-start(f32[1,4,1,128]{3,2,1,0:T(1,128)} %param.16) | copy-start | bytes 6148
  4.9 3.8 %collective-permute-start.1 = (f32[32,128]{1,0:T(8,128)S(1)}, f32[32,128]{1,0:T(8,128)S(1)}, u32[]{:S(2)}, u32[]{:S(2)}) collective-permute-start(f32[32,128]{1,0:T(8,128)S(1)} %edge.1), channel_id=1, source_target_pairs={{0,16},{16,0},{1,17},{17,1},{2,18},{18,2},{3,19},{19,3},{4,20},{20... | collective-permute-start | bytes 49160 | tf_op jit(solution)/shard_map/ppermute | solution.py:807
  9.0 8.6 %collective-permute-start.3 = (f32[88,128]{1,0:T(8,128)S(1)}, f32[88,128]{1,0:T(8,128)S(1)}, u32[]{:S(2)}, u32[]{:S(2)}) collective-permute-start(f32[88,128]{1,0:T(8,128)S(1)} %get-tuple-element.52), channel_id=1, source_target_pairs={{2,1},{3,0},{6,5},{7,4},{10,9},{11,8},{14,13},{15,12},{18,17},{19,... | collective-permute-start | bytes 135176 | tf_op jit(solution)/shard_map/ppermute | solution.py:878
  10.3 8.6 %collective-permute-start.4 = (f32[96,128]{1,0:T(8,128)S(1)}, f32[96,128]{1,0:T(8,128)S(1)}, u32[]{:S(2)}, u32[]{:S(2)}) collective-permute-start(f32[96,128]{1,0:T(8,128)S(1)} %get-tuple-element.53), channel_id=1, source_target_pairs={{0,2},{1,3},{2,0},{3,1},{4,6},{5,7},{6,4},{7,5},{8,10},{9,11},{10,... | collective-permute-start | bytes 147464 | tf_op jit(solution)/shard_map/ppermute | solution.py:751
  14.0 4.9 %collective-permute-start.5 = (f32[96,128]{1,0:T(8,128)S(1)}, f32[96,128]{1,0:T(8,128)S(1)}, u32[]{:S(2)}, u32[]{:S(2)}) collective-permute-start(f32[96,128]{1,0:T(8,128)S(1)} %get-tuple-element.54), channel_id=1, source_target_pairs={{1,2},{0,3},{5,6},{4,7},{9,10},{8,11},{13,14},{12,15},{17,18},{16,... | collective-permute-start | bytes 147464 | tf_op jit(solution)/shard_map/ppermute | solution.py:879
  16.8 4.2 %collective-permute-start.6 = (f32[96,128]{1,0:T(8,128)S(1)}, f32[96,128]{1,0:T(8,128)S(1)}, u32[]{:S(2)}, u32[]{:S(2)}) collective-permute-start(f32[96,128]{1,0:T(8,128)S(1)} %get-tuple-element.55), channel_id=1, source_target_pairs={{0,1},{1,0},{2,3},{3,2},{4,5},{5,4},{6,7},{7,6},{8,9},{9,8},{10,11... | collective-permute-start | bytes 147464 | tf_op jit(solution)/shard_map/ppermute | solution.py:751
  17.1 7.6 %collective-permute-start.10 = (f32[160,128]{1,0:T(8,128)S(1)}, f32[160,128]{1,0:T(8,128)S(1)}, u32[]{:S(2)}, u32[]{:S(2)}) collective-permute-start(f32[160,128]{1,0:T(8,128)S(1)} %get-tuple-element.63), channel_id=1, source_target_pairs={{0,12},{4,8},{8,4},{12,0},{1,13},{5,9},{9,5},{13,1},{2,14},{6,10},... | collective-permute-start | bytes 245768 | tf_op jit(solution)/shard_map/ppermute | solution.py:890
  17.6 7.1 %collective-permute-start.11 = (f32[160,128]{1,0:T(8,128)S(1)}, f32[160,128]{1,0:T(8,128)S(1)}, u32[]{:S(2)}, u32[]{:S(2)}) collective-permute-start(f32[160,128]{1,0:T(8,128)S(1)} %get-tuple-element.64), channel_id=1, source_target_pairs={{0,12},{4,8},{8,4},{12,0},{1,13},{5,9},{9,5},{13,1},{2,14},{6,10},... | collective-permute-start | bytes 245768 | tf_op jit(solution)/shard_map/ppermute | solution.py:890
  21.2 5.4 %collective-permute-start.8 = (f32[88,128]{1,0:T(8,128)S(1)}, f32[88,128]{1,0:T(8,128)S(1)}, u32[]{:S(2)}, u32[]{:S(2)}) collective-permute-start(f32[88,128]{1,0:T(8,128)S(1)} %bitcast.33), channel_id=1, source_target_pairs={{0,2},{1,3},{2,0},{3,1},{4,6},{5,7},{6,4},{7,5},{8,10},{9,11},{10,... | collective-permute-start | bytes 135176 | tf_op jit(solution)/shard_map/ppermute | solution.py:751
  21.2 6.0 %collective-permute-start.7 = (f32[88,128]{1,0:T(8,128)S(1)}, f32[88,128]{1,0:T(8,128)S(1)}, u32[]{:S(2)}, u32[]{:S(2)}) collective-permute-start(f32[88,128]{1,0:T(8,128)S(1)} %bitcast.32), channel_id=1, source_target_pairs={{0,3},{1,2},{2,1},{3,0},{4,7},{5,6},{6,5},{7,4},{8,11},{9,10},{10,... | collective-permute-start | bytes 135176 | tf_op jit(solution)/shard_map/ppermute | solution.py:751
  24.0 4.0 %collective-permute-start.9 = (f32[88,128]{1,0:T(8,128)S(1)}, f32[88,128]{1,0:T(8,128)S(1)}, u32[]{:S(2)}, u32[]{:S(2)}) collective-permute-start(f32[88,128]{1,0:T(8,128)S(1)} %bitcast.31), channel_id=1, source_target_pairs={{0,1},{1,0},{2,3},{3,2},{4,5},{5,4},{6,7},{7,6},{8,9},{9,8},{10,11... | collective-permute-start | bytes 135176 | tf_op jit(solution)/shard_map/ppermute | solution.py:751

commit v2 on v0

--- a/solution.py
+++ b/solution.py
@@ -88,10 +88,6 @@
 
 def side_sign(side):
     return (2 * side - 1).astype(jnp.float32)
-
-
-def ends(total):
-    return list(range(0, total, ROWS))
 
 
 def pick(values, masks, flip):
@@ -176,10 +172,16 @@
                 state_hbm.at[:, rows, :], state.at[:, rows, :], semaphores.at[len(small) + place]
             )
         )
-    for copy in small[:1] + large + small[1:]:
+    for copy in (small[0], small[5], *large, *small[1:5]):
         copy.start()
     column[...] = jnp.zeros_like(column)
     small[0].wait()
+    small[5].wait()
+    for place, source in enumerate((flux, second_flux)):
+        for f in range(FIELDS):
+            for g in range(FIELDS):
+                at = flux_row(f, g, place)
+                fluxes[at : at + 1, :] = jnp.full((1, lanes), source[f, g])
     arrived = 0
     for piece, start in enumerate(chunks(levels)):
         while arrived < len(groups) and groups[arrived][0] < start + ROWS:
@@ -214,12 +216,6 @@
     to_other[end + 2 :, :] = jnp.zeros((left, lanes), jnp.float32)
     small[3].wait()
     small[4].wait()
-    small[5].wait()
-    for place, source in enumerate((flux, second_flux)):
-        for f in range(FIELDS):
-            for g in range(FIELDS):
-                at = flux_row(f, g, place)
-                fluxes[at : at + 1, :] = jnp.full((1, lanes), source[f, g])
 
 
 def edge_kernel(state, to_sides):
@@ -279,10 +275,9 @@
         for k in range(NODES):
             at = (levels + extra) * NODES + k
             source[at : at + 1, :] = column[k, ROWS + level : ROWS + level + 1, :]
-    half[...] = base[...]
     for start in chunks(levels + 2):
         picked = [source[pl.ds(start * NODES + k, ROWS, stride=NODES), :] for k in range(NODES)]
-        add_first_side(0, start, picked, half, base, metric)
+        add_first_side(0, start, picked, half, metric)
 
 
 def face_kernel(partner, state, received, fluxes, *rest):
@@ -444,13 +439,18 @@
     return pick(values, masks, flip)
 
 
-def add_first_side(partner, start, picked, send, base, metric):
+def add_first_side(partner, start, picked, send, metric):
     weight = 0.5 * lift_weight * step_size
     i = (NODES - 1) * partner_side(partner)
+    fresh = fresh_rows(start, picked[0].shape)
     for j, row in enumerate(picked):
         at = pl.ds(start * NODES + i, ROWS, stride=NODES)
         scale = weight * metric[pl.ds(NODES * j + i, 1), :]
-        send[j, at, :] = base[j, at, :] + scale * row
+        send[j, at, :] += jnp.where(fresh, scale * row, 0.0)
+
+
+def fresh_rows(start, shape):
+    return lax.broadcasted_iota(jnp.int32, shape, 0) >= (-start) % ROWS
 
 
 def pack_kernel(half, from_other, neighbour_face, orientation, metric, *rest):
@@ -468,7 +468,7 @@
             point: from_other[pl.ds(start * width + place, ROWS, stride=width), :]
             for place, point in enumerate(RIM_POINTS)
         }
-        add_first_side(1, start, pick(values, masks, flip), send, half, metric)
+        add_first_side(1, start, pick(values, masks, flip), send, metric)
     for out, way in zip(sends, WAYS):
         out[...] = send[me ^ way]
 
@@ -483,7 +483,6 @@
     fluxes,
     factored,
     half,
-    send,
     column,
     mixed,
 ):
@@ -491,8 +490,6 @@
     levels = rows // NODES - 2
     width = len(RIM_POINTS)
     weight = 0.5 * lift_weight * step_size
-    send[:, 0:rows, :] = base[...]
-    send[:, rows:, :] = jnp.zeros((NODES, send.shape[1] - rows, lanes), jnp.float32)
     column[...] = jnp.zeros_like(column)
     mixed[...] = jnp.zeros_like(mixed)
     lane = lax.broadcasted_iota(jnp.int32, (ROWS, lanes), 1)
@@ -512,14 +509,14 @@
             mixed[pl.ds(start, ROWS), :] = value - gravity_couple * (upper - lower)
         mixed[levels : levels + 1, :] = column[ROWS : ROWS + 1, :]
         mixed[levels + 1 : levels + 2, :] = column[ROWS + levels - 1 : ROWS + levels, :]
-        for start in ends(levels + 2):
+        for start in chunks(levels + 2):
+            fresh = (lane == edge) & fresh_rows(start, lane.shape)
             picked = spread(mixed[start : start + ROWS, :], edge, masks, flip)
             for k, row in enumerate(picked):
                 point = NODES * j + k
                 at = pl.ds(start * NODES + k, ROWS, stride=NODES)
                 scale = weight * metric[point : point + 1, :]
-                send[j, at, :] += jnp.where(lane == edge, scale * row, 0.0)
-    half[...] = send[:, 0:rows, :]
+                half[j, at, :] += jnp.where(fresh, scale * row, 0.0)
 
 
 def finish_section_kernel(
@@ -708,7 +705,7 @@
 ANY = pl.BlockSpec(memory_space=pl.ANY)
 
 
-def call(kernel, outs, in_specs, scratch=(), cost=0, name=None):
+def call(kernel, outs, in_specs, scratch=(), cost=0, name=None, aliases=None):
     kinds = [x if hasattr(x, "dtype") else pltpu.VMEM(x, jnp.float32) for x in outs]
     return pl.pallas_call(
         kernel,
@@ -716,6 +713,7 @@
         in_specs=in_specs,
         out_specs=[VMEM] * len(outs),
         scratch_shapes=list(scratch),
+        input_output_aliases=aliases or {},
         compiler_params=pltpu.CompilerParams(vmem_limit_bytes=24 * 1024 * 1024),
         cost_estimate=pl.CostEstimate(flops=cost, bytes_accessed=cost, transcendentals=0),
         name=name,
@@ -836,6 +834,7 @@
         [pltpu.VMEM((NODES, padded, lanes), jnp.float32), pltpu.VMEM(block, jnp.float32)],
         cost=1000,
         name="near",
+        aliases={4: 0},
     )(from_near, neighbour_face, orientation, fluxes, base, metric)
     count = -(-(levels + 2) // ROWS) * ROWS
     (half,) = call(
@@ -843,12 +842,12 @@
         [(NODES,) + block],
         [VMEM] * 7 + [ANY],
         [
-            pltpu.VMEM((NODES, count * NODES, lanes), jnp.float32),
             pltpu.VMEM((padded, lanes), jnp.float32),
             pltpu.VMEM((count, lanes), jnp.float32),
         ],
         cost=1000,
         name="half_pack",
+        aliases={0: 0},
     )(
         base,
         from_down,

time: 26.1 us -> 26 us (level)
  no operation moved by 1% of the time
where the time goes in v2:
time: 26 us; the launch traced here: 25.9 us
  starting transfers between devices  14.3 us (55%)
  Pallas kernels  6.52 us (25%)
  waiting for transfers between devices  4.98 us (19%)
    ppermute x6, starting transfers between devices, exchange(): lax.ppermute(x, 'vz', [(i, i ^ way) for i in range(size)])  7.79 us
    ppermute x6, waiting for transfers between devices, exchange(): lax.ppermute(x, 'vz', [(i, i ^ way) for i in range(size)])  4.59 us
    ppermute x1, starting transfers between devices, per_device(): from_other = lax.ppermute(to_other, 'hy', other)  2.64 us
    ppermute x2, starting transfers between devices, per_device(): other_face = [lax.ppermute(x, 'hy', other) for x in other_face]  1.81 us
    ppermute x1, starting transfers between devices, per_device(): from_down = lax.ppermute(to_sides, 'hx', second_up)  1.56 us
    pallas_call x1, Pallas kernels, per_device(): call(rim_kernel, [message, whole, table, table, (POINTS, lanes), tables.s...  1.41 us
    pallas_call x1, Pallas kernels, per_device(): pl.pallas_call(finish_section_kernel, out_shape=[jax.ShapeDtypeStruct(who...  1.33 us
    pallas_call x1, Pallas kernels, per_device(): pl.pallas_call(update_kernel, out_shape=jax.ShapeDtypeStruct(whole, jnp.f...  0.88 us
  transfers between devices with their start and end apart: 11, of which 4 were waited for; matrix products, arithmetic and copies ran while one was open for 0% of the time, Pallas kernels for 16%

profile of v2, /device:TPU:0, one launch (start us, length us, event | category | flops | bytes accessed | tf_op | source)
XLA Modules:
  0.0 25.9 jit_solution(17224991686711557082)
XLA Ops:
  0.0 0.0 copy-start
  0.0 1.4 %rim.1 = (f32[272,128]{1,0:T(8,128)S(1)}, f32[5,320,128]{2,1,0:T(8,128)S(1)}, s32[4,128]{1,0:T(4,128)S(1)}, s32[4,128]{1,0:T(4,128)S(1)}, f32[16,128]{1,0:T(8,12...) custom-call(f32[5,320,128]{2,1,0:T(8,128)} %bitcast.32, s32[4,128]{1,0:T(4,128)} %bitcast.34, s32[4,128]{1,0:T(4,128)} %bitcast.35, ...), custom_call_target="tpu_custom_call" | custom-call | flops 1000 | bytes 1000 | tf_op jit(solution)/shard_map/rim/pallas_call | solution.py:774
  1.4 0.5 %collective-permute-start = (f32[1600,128]{1,0:T(8,128)S(1)}, f32[1600,128]{1,0:T(8,128)S(1)}, u32[]{:S(2)}, u32[]{:S(2)}) collective-permute-start(f32[1600,128]{1,0:T(8,128)S(1)} %bitcast.18), channel_id=1, source_target_pairs={{0,4},{4,0},{8,12},{12,8},{1,5},{5,1},{9,13},{13,9},{2,6},{6,2},{1... | collective-permute-start | bytes 2457608 | tf_op jit(solution)/shard_map/ppermute | solution.py:798
  1.9 2.6 %collective-permute-start.2 = (f32[272,128]{1,0:T(8,128)S(1)}, f32[272,128]{1,0:T(8,128)S(1)}, u32[]{:S(2)}, u32[]{:S(2)}) collective-permute-start(f32[272,128]{1,0:T(8,128)S(1)} %get-tuple-element.50), channel_id=1, source_target_pairs={{0,12},{4,8},{8,4},{12,0},{1,13},{5,9},{9,5},{13,1},{2,14},{6,10},... | collective-permute-start | bytes 417800 | tf_op jit(solution)/shard_map/ppermute | solution.py:797
  4.6 0.3 %edge.1 = f32[32,128]{1,0:T(8,128)S(1)} custom-call(f32[1600,128]{1,0:T(8,128)S(1)} %bitcast.19), custom_call_target="tpu_custom_call" | custom-call | flops 1000 | bytes 1000 | tf_op jit(solution)/shard_map/edge/pallas_call | solution.py:799
  4.9 0.0 copy-start.1
  4.9 1.6 %collective-permute-start.1 = (f32[32,128]{1,0:T(8,128)S(1)}, f32[32,128]{1,0:T(8,128)S(1)}, u32[]{:S(2)}, u32[]{:S(2)}) collective-permute-start(f32[32,128]{1,0:T(8,128)S(1)} %edge.1), channel_id=1, source_target_pairs={{0,16},{16,0},{1,17},{17,1},{2,18},{18,2},{3,19},{19,3},{4,20},{20... | collective-permute-start | bytes 49160 | tf_op jit(solution)/shard_map/ppermute | solution.py:800
  6.4 0.0 copy-done
  6.4 0.0 copy-done.1
  6.4 0.7 %factor.1 = (f32[80,4,128]{2,1,0:T(4,128)S(1)}, f32[80,4,128]{2,1,0:T(4,128)S(1)}, f32[80,4,128]{2,1,0:T(4,128)S(1)}, f32[80,4,128]{2,1,0:T(4,128)S(1)}, f32[80,...) custom-call(f32[4,80,4,128]{3,2,1,0:T(4,128)S(1)} %bitcast.22, f32[4,128]{1,0:T(4,128)S(1)} %bitcast.28), custom_call_target="tpu_custom_call" | custom-call | flops 4000000 | bytes 4000000 | tf_op jit(solution)/shard_map/factor/pallas_call | solution.py:806
  7.2 0.8 %element.1 = (f32[1600,128]{1,0:T(8,128)S(1)}, f32[4,88,128]{2,1,0:T(8,128)S(1)}) custom-call(f32[1600,128]{1,0:T(8,128)S(1)} %bitcast.20, s32[4,128]{1,0:T(4,128)S(1)} %get-tuple-element.43.neighbour_face, s32[4,128]{1,0:T(4,128)S(1)} %get-tuple-element.44.orientation, f32[16,128]{1,0:T(8,128)S(1)} %get-tuple-element.46.metric, ...), custom_call_target="tpu_custom_call" | custom-call | flops 4000000 | bytes 4000000 | tf_op jit(solution)/shard_map/element/pallas_call | solution.py:810
  8.0 0.0 collective-permute-done.state
  8.0 0.3 %near.1 = (f32[4,88,128]{2,1,0:T(8,128)S(1)}, f32[320,128]{1,0:T(8,128)S(1)}) custom-call(f32[1600,128]{1,0:T(8,128)S(1)} %collective-permute-done.state, s32[4,128]{1,0:T(4,128)S(1)} %get-tuple-element.43.neighbour_face, s32[4,128]{1,0:T(4,128)S(1)} %get-tuple-element.44.orientation, ...), custom_call_target="tpu_custom_call", output_to_operand_aliasing={{0}: (4, {})} | custom-call | flops 1000 | bytes 1000 | tf_op jit(solution)/shard_map/near/pallas_call | solution.py:830
  8.3 0.4 %collective-permute-done.1.from_down.from_up = f32[32,128]{1,0:T(8,128)S(1)} collective-permute-done((f32[32,128]{1,0:T(8,128)S(1)}, f32[32,128]{1,0:T(8,128)S(1)}, u32[]{:S(2)}, u32[]{:S(2)}) %collective-permute-start.1) | collective-permute-done | bytes 16416 | tf_op jit(solution)/shard_map/ppermute | solution.py:800
  8.7 0.2 half_pack.1.half
  8.9 0.0 collective-permute-done.2.from_other.received
  8.9 0.1 pack.1
  9.0 2.7 %collective-permute-start.3 = (f32[88,128]{1,0:T(8,128)S(1)}, f32[88,128]{1,0:T(8,128)S(1)}, u32[]{:S(2)}, u32[]{:S(2)}) collective-permute-start(f32[88,128]{1,0:T(8,128)S(1)} %get-tuple-element.51), channel_id=1, source_target_pairs={{0,2},{1,3},{2,0},{3,1},{4,6},{5,7},{6,4},{7,5},{8,10},{9,11},{10,... | collective-permute-start | bytes 135176 | tf_op jit(solution)/shard_map/ppermute | solution.py:744
  11.6 1.3 %collective-permute-start.4 = (f32[88,128]{1,0:T(8,128)S(1)}, f32[88,128]{1,0:T(8,128)S(1)}, u32[]{:S(2)}, u32[]{:S(2)}) collective-permute-start(f32[88,128]{1,0:T(8,128)S(1)} %get-tuple-element.52), channel_id=1, source_target_pairs={{0,3},{1,2},{2,1},{3,0},{4,7},{5,6},{6,5},{7,4},{8,11},{9,10},{10,... | collective-permute-start | bytes 135176 | tf_op jit(solution)/shard_map/ppermute | solution.py:744
  13.0 0.2 collective-permute-start.5
  13.2 0.3 other_face.1
  13.5 0.5 %collective-permute-start.9 = (f32[160,128]{1,0:T(8,128)S(1)}, f32[160,128]{1,0:T(8,128)S(1)}, u32[]{:S(2)}, u32[]{:S(2)}) collective-permute-start(f32[160,128]{1,0:T(8,128)S(1)} %get-tuple-element.61), channel_id=1, source_target_pairs={{0,12},{4,8},{8,4},{12,0},{1,13},{5,9},{9,5},{13,1},{2,14},{6,10},... | collective-permute-start | bytes 245768 | tf_op jit(solution)/shard_map/ppermute | solution.py:878
  14.0 1.3 %collective-permute-start.10 = (f32[160,128]{1,0:T(8,128)S(1)}, f32[160,128]{1,0:T(8,128)S(1)}, u32[]{:S(2)}, u32[]{:S(2)}) collective-permute-start(f32[160,128]{1,0:T(8,128)S(1)} %get-tuple-element.62), channel_id=1, source_target_pairs={{0,12},{4,8},{8,4},{12,0},{1,13},{5,9},{9,5},{13,1},{2,14},{6,10},... | collective-permute-start | bytes 245768 | tf_op jit(solution)/shard_map/ppermute | solution.py:878
  15.3 0.0 collective-permute-done.3
  15.3 2.2 %collective-permute-done.4 = f32[88,128]{1,0:T(8,128)S(1)} collective-permute-done((f32[88,128]{1,0:T(8,128)S(1)}, f32[88,128]{1,0:T(8,128)S(1)}, u32[]{:S(2)}, u32[]{:S(2)}) %collective-permute-start.4) | collective-permute-done | bytes 45088 | tf_op jit(solution)/shard_map/ppermute | solution.py:744
  17.5 0.0 collective-permute-done.5
  17.5 0.2 solve.1
  17.8 1.4 %collective-permute-start.7 = (f32[88,128]{1,0:T(8,128)S(1)}, f32[88,128]{1,0:T(8,128)S(1)}, u32[]{:S(2)}, u32[]{:S(2)}) collective-permute-start(f32[88,128]{1,0:T(8,128)S(1)} %bitcast.31), channel_id=1, source_target_pairs={{0,2},{1,3},{2,0},{3,1},{4,6},{5,7},{6,4},{7,5},{8,10},{9,11},{10,... | collective-permute-start | bytes 135176 | tf_op jit(solution)/shard_map/ppermute | solution.py:744
  19.2 1.1 %collective-permute-start.6 = (f32[88,128]{1,0:T(8,128)S(1)}, f32[88,128]{1,0:T(8,128)S(1)}, u32[]{:S(2)}, u32[]{:S(2)}) collective-permute-start(f32[88,128]{1,0:T(8,128)S(1)} %bitcast.30), channel_id=1, source_target_pairs={{0,3},{1,2},{2,1},{3,0},{4,7},{5,6},{6,5},{7,4},{8,11},{9,10},{10,... | collective-permute-start | bytes 135176 | tf_op jit(solution)/shard_map/ppermute | solution.py:744
  20.3 1.0 %collective-permute-start.8 = (f32[88,128]{1,0:T(8,128)S(1)}, f32[88,128]{1,0:T(8,128)S(1)}, u32[]{:S(2)}, u32[]{:S(2)}) collective-permute-start(f32[88,128]{1,0:T(8,128)S(1)} %bitcast.29), channel_id=1, source_target_pairs={{0,1},{1,0},{2,3},{3,2},{4,5},{5,4},{6,7},{7,6},{8,9},{9,8},{10,11... | collective-permute-start | bytes 135176 | tf_op jit(solution)/shard_map/ppermute | solution.py:744
  21.3 0.0 collective-permute-done.9.other_early
  21.3 0.0 collective-permute-done.10.other_late
  21.3 1.3 %finish.1 = (f32[5,320,128]{2,1,0:T(8,128)}, f32[2,320,128]{2,1,0:T(8,128)S(1)}) custom-call(f32[1600,128]{1,0:T(8,128)S(1)} %get-tuple-element.59.part, f32[320,128]{1,0:T(8,128)S(1)} %get-tuple-element.60.near, f32[160,128]{1,0:T(8,128)S(1)} %collective-permute-done.9.other_early, f32[160,128]{1,0:T(8,128)S(1)} %collective-permute-done.10.other_late, ...), custom_call_target="tpu_custom_call" | custom-call | flops 4000000 | bytes 4000000 | tf_op jit(solution)/shard_map/finish/pallas_call | solution.py:896
  22.7 0.6 %collective-permute-done.7.refs_1_ = f32[88,128]{1,0:T(8,128)S(1)} collective-permute-done((f32[88,128]{1,0:T(8,128)S(1)}, f32[88,128]{1,0:T(8,128)S(1)}, u32[]{:S(2)}, u32[]{:S(2)}) %collective-permute-start.7) | collective-permute-done | bytes 45088 | tf_op jit(solution)/shard_map/ppermute | solution.py:744
  23.3 1.8 %collective-permute-done.6.refs_0_ = f32[88,128]{1,0:T(8,128)S(1)} collective-permute-done((f32[88,128]{1,0:T(8,128)S(1)}, f32[88,128]{1,0:T(8,128)S(1)}, u32[]{:S(2)}, u32[]{:S(2)}) %collective-permute-start.6) | collective-permute-done | bytes 45088 | tf_op jit(solution)/shard_map/ppermute | solution.py:744
  25.0 0.0 collective-permute-done.8.refs_2_
  25.0 0.9 %update.1 = f32[5,320,128]{2,1,0:T(8,128)} custom-call(f32[88,128]{1,0:T(8,128)S(1)} %collective-permute-done.6.refs_0_, f32[88,128]{1,0:T(8,128)S(1)} %collective-permute-done.7.refs_1_, f32[88,128]{1,0:T(8,128)S(1)} %collective-permute-done.8.refs_2_, f32[88,128]{1,0:T(8,128)S(1)} %bitcast.24, ...), custom_call_target="tpu_custom_call", output_to_operand_aliasing={{}: (5, {})} | custom-call | tf_op jit(solution)/shard_map/update/pallas_call | solution.py:914
Async XLA Ops:
  0.0 6.4 %copy-start = (f32[4,80,1,4,1,128]{5,4,3,2,1,0:T(1,128)S(1)}, f32[4,80,1,4,1,128]{5,4,3,2,1,0:T(1,128)}, u32[]{:S(2)}) copy-start(f32[4,80,1,4,1,128]{5,4,3,2,1,0:T(1,128)} %param.15) | copy-start | bytes 1966084
  1.4 6.6 %collective-permute-start = (f32[1600,128]{1,0:T(8,128)S(1)}, f32[1600,128]{1,0:T(8,128)S(1)}, u32[]{:S(2)}, u32[]{:S(2)}) collective-permute-start(f32[1600,128]{1,0:T(8,128)S(1)} %bitcast.18), channel_id=1, source_target_pairs={{0,4},{4,0},{8,12},{12,8},{1,5},{5,1},{9,13},{13,9},{2,6},{6,2},{1... | collective-permute-start | bytes 2457608 | tf_op jit(solution)/shard_map/ppermute | solution.py:798
  1.9 7.0 %collective-permute-start.2 = (f32[272,128]{1,0:T(8,128)S(1)}, f32[272,128]{1,0:T(8,128)S(1)}, u32[]{:S(2)}, u32[]{:S(2)}) collective-permute-start(f32[272,128]{1,0:T(8,128)S(1)} %get-tuple-element.50), channel_id=1, source_target_pairs={{0,12},{4,8},{8,4},{12,0},{1,13},{5,9},{9,5},{13,1},{2,14},{6,10},... | collective-permute-start | bytes 417800 | tf_op jit(solution)/shard_map/ppermute | solution.py:797
  4.9 1.6 %copy-start.1 = (f32[1,4,1,128]{3,2,1,0:T(1,128)S(1)}, f32[1,4,1,128]{3,2,1,0:T(1,128)}, u32[]{:S(2)}) copy-start(f32[1,4,1,128]{3,2,1,0:T(1,128)} %param.16) | copy-start | bytes 6148
  4.9 3.8 %collective-permute-start.1 = (f32[32,128]{1,0:T(8,128)S(1)}, f32[32,128]{1,0:T(8,128)S(1)}, u32[]{:S(2)}, u32[]{:S(2)}) collective-permute-start(f32[32,128]{1,0:T(8,128)S(1)} %edge.1), channel_id=1, source_target_pairs={{0,16},{16,0},{1,17},{17,1},{2,18},{18,2},{3,19},{19,3},{4,20},{20... | collective-permute-start | bytes 49160 | tf_op jit(solution)/shard_map/ppermute | solution.py:800
  9.0 6.3 %collective-permute-start.3 = (f32[88,128]{1,0:T(8,128)S(1)}, f32[88,128]{1,0:T(8,128)S(1)}, u32[]{:S(2)}, u32[]{:S(2)}) collective-permute-start(f32[88,128]{1,0:T(8,128)S(1)} %get-tuple-element.51), channel_id=1, source_target_pairs={{0,2},{1,3},{2,0},{3,1},{4,6},{5,7},{6,4},{7,5},{8,10},{9,11},{10,... | collective-permute-start | bytes 135176 | tf_op jit(solution)/shard_map/ppermute | solution.py:744
  11.6 5.9 %collective-permute-start.4 = (f32[88,128]{1,0:T(8,128)S(1)}, f32[88,128]{1,0:T(8,128)S(1)}, u32[]{:S(2)}, u32[]{:S(2)}) collective-permute-start(f32[88,128]{1,0:T(8,128)S(1)} %get-tuple-element.52), channel_id=1, source_target_pairs={{0,3},{1,2},{2,1},{3,0},{4,7},{5,6},{6,5},{7,4},{8,11},{9,10},{10,... | collective-permute-start | bytes 135176 | tf_op jit(solution)/shard_map/ppermute | solution.py:744
  13.0 4.5 %collective-permute-start.5 = (f32[88,128]{1,0:T(8,128)S(1)}, f32[88,128]{1,0:T(8,128)S(1)}, u32[]{:S(2)}, u32[]{:S(2)}) collective-permute-start(f32[88,128]{1,0:T(8,128)S(1)} %get-tuple-element.53), channel_id=1, source_target_pairs={{0,1},{1,0},{2,3},{3,2},{4,5},{5,4},{6,7},{7,6},{8,9},{9,8},{10,11... | collective-permute-start | bytes 135176 | tf_op jit(solution)/shard_map/ppermute | solution.py:744
  13.5 7.9 %collective-permute-start.9 = (f32[160,128]{1,0:T(8,128)S(1)}, f32[160,128]{1,0:T(8,128)S(1)}, u32[]{:S(2)}, u32[]{:S(2)}) collective-permute-start(f32[160,128]{1,0:T(8,128)S(1)} %get-tuple-element.61), channel_id=1, source_target_pairs={{0,12},{4,8},{8,4},{12,0},{1,13},{5,9},{9,5},{13,1},{2,14},{6,10},... | collective-permute-start | bytes 245768 | tf_op jit(solution)/shard_map/ppermute | solution.py:878
  14.0 7.4 %collective-permute-start.10 = (f32[160,128]{1,0:T(8,128)S(1)}, f32[160,128]{1,0:T(8,128)S(1)}, u32[]{:S(2)}, u32[]{:S(2)}) collective-permute-start(f32[160,128]{1,0:T(8,128)S(1)} %get-tuple-element.62), channel_id=1, source_target_pairs={{0,12},{4,8},{8,4},{12,0},{1,13},{5,9},{9,5},{13,1},{2,14},{6,10},... | collective-permute-start | bytes 245768 | tf_op jit(solution)/shard_map/ppermute | solution.py:878
  17.8 5.5 %collective-permute-start.7 = (f32[88,128]{1,0:T(8,128)S(1)}, f32[88,128]{1,0:T(8,128)S(1)}, u32[]{:S(2)}, u32[]{:S(2)}) collective-permute-start(f32[88,128]{1,0:T(8,128)S(1)} %bitcast.31), channel_id=1, source_target_pairs={{0,2},{1,3},{2,0},{3,1},{4,6},{5,7},{6,4},{7,5},{8,10},{9,11},{10,... | collective-permute-start | bytes 135176 | tf_op jit(solution)/shard_map/ppermute | solution.py:744
  19.2 5.8 %collective-permute-start.6 = (f32[88,128]{1,0:T(8,128)S(1)}, f32[88,128]{1,0:T(8,128)S(1)}, u32[]{:S(2)}, u32[]{:S(2)}) collective-permute-start(f32[88,128]{1,0:T(8,128)S(1)} %bitcast.30), channel_id=1, source_target_pairs={{0,3},{1,2},{2,1},{3,0},{4,7},{5,6},{6,5},{7,4},{8,11},{9,10},{10,... | collective-permute-start | bytes 135176 | tf_op jit(solution)/shard_map/ppermute | solution.py:744
  20.3 4.7 %collective-permute-start.8 = (f32[88,128]{1,0:T(8,128)S(1)}, f32[88,128]{1,0:T(8,128)S(1)}, u32[]{:S(2)}, u32[]{:S(2)}) collective-permute-start(f32[88,128]{1,0:T(8,128)S(1)} %bitcast.29), channel_id=1, source_target_pairs={{0,1},{1,0},{2,3},{3,2},{4,5},{5,4},{6,7},{7,6},{8,9},{9,8},{10,11... | collective-permute-start | bytes 135176 | tf_op jit(solution)/shard_map/ppermute | solution.py:744

commit v3 on v0

--- a/solution.py
+++ b/solution.py
@@ -668,6 +668,7 @@
         speed[me ^ way] = values[...]
     lanes = done.shape[2]
     half = levels // 2
+    early = (7 * half) // 10
     low = lax.broadcasted_iota(jnp.int32, (ROWS, lanes), 0) < NODES
     copies = []
     for pair in range(half):
@@ -683,13 +684,15 @@
                 final[0, at, :] = done[0, at, :] - density_couple * jumps
                 final[1, at, :] = side_by_side(value[a], value[b], 1 - odd, low)
                 final[2, at, :] = done[1, at, :] - theta_couple * jumps
-        if pair in (half // 2 - 1, half - 1):
-            first = 0 if pair < half - 1 else half // 2
+        if pair in (early - 1, half - 1):
+            first = 0 if pair < half - 1 else early
             rows = pl.ds(first * 2 * POINTS, (pair + 1 - first) * 2 * POINTS)
-            for place, f in enumerate((0, 3, 4)):
+            for place, f, count in ((1, 3, 2), (0, 0, 1)):
                 copies.append(
                     pltpu.make_async_copy(
-                        final.at[place, rows, :], out.at[f, rows, :], semaphores.at[len(copies)]
+                        final.at[place : place + count, rows, :],
+                        out.at[f : f + count, rows, :],
+                        semaphores.at[len(copies)],
                     )
                 )
                 copies[-1].start()
@@ -921,7 +924,7 @@
         scratch_shapes=[
             pltpu.VMEM((NODES,) + block, jnp.float32),
             pltpu.VMEM((3, size, lanes), jnp.float32),
-            pltpu.SemaphoreType.DMA((6,)),
+            pltpu.SemaphoreType.DMA((4,)),
         ],
         compiler_params=limits,
         name="update",

time: 26.1 us -> 26.1 us (level)
  no operation moved by 1% of the time
where the time goes in v3:
time: 26.1 us; the launch traced here: 25.9 us
  starting transfers between devices  14.3 us (55%)
  Pallas kernels  6.54 us (25%)
  waiting for transfers between devices  4.97 us (19%)
    ppermute x6, starting transfers between devices, exchange(): lax.ppermute(x, 'vz', [(i, i ^ way) for i in range(size)])  7.79 us
    ppermute x6, waiting for transfers between devices, exchange(): lax.ppermute(x, 'vz', [(i, i ^ way) for i in range(size)])  4.58 us
    ppermute x1, starting transfers between devices, per_device(): from_other = lax.ppermute(to_other, 'hy', other)  2.64 us
    ppermute x2, starting transfers between devices, per_device(): other_face = [lax.ppermute(x, 'hy', other) for x in other_face]  1.81 us
    ppermute x1, starting transfers between devices, per_device(): from_down = lax.ppermute(to_sides, 'hx', second_up)  1.56 us
    pallas_call x1, Pallas kernels, per_device(): call(rim_kernel, [message, whole, table, table, (POINTS, lanes), tables.s...  1.44 us
    pallas_call x1, Pallas kernels, per_device(): pl.pallas_call(finish_section_kernel, out_shape=[jax.ShapeDtypeStruct(who...  1.33 us
    pallas_call x1, Pallas kernels, per_device(): pl.pallas_call(update_kernel, out_shape=jax.ShapeDtypeStruct(whole, jnp.f...  0.87 us
  transfers between devices with their start and end apart: 11, of which 4 were waited for; matrix products, arithmetic and copies ran while one was open for 0% of the time, Pallas kernels for 16%

profile of v3, /device:TPU:0, one launch (start us, length us, event | category | flops | bytes accessed | tf_op | source)
XLA Modules:
  0.0 25.9 jit_solution(9081834924696373738)
XLA Ops:
  0.0 0.0 copy-start
  0.0 1.4 %rim.1 = (f32[272,128]{1,0:T(8,128)S(1)}, f32[5,320,128]{2,1,0:T(8,128)S(1)}, s32[4,128]{1,0:T(4,128)S(1)}, s32[4,128]{1,0:T(4,128)S(1)}, f32[16,128]{1,0:T(8,12...) custom-call(f32[5,320,128]{2,1,0:T(8,128)} %bitcast.32, s32[4,128]{1,0:T(4,128)} %bitcast.34, s32[4,128]{1,0:T(4,128)} %bitcast.35, ...), custom_call_target="tpu_custom_call" | custom-call | flops 1000 | bytes 1000 | tf_op jit(solution)/shard_map/rim/pallas_call | solution.py:779
  1.4 0.5 %collective-permute-start = (f32[1600,128]{1,0:T(8,128)S(1)}, f32[1600,128]{1,0:T(8,128)S(1)}, u32[]{:S(2)}, u32[]{:S(2)}) collective-permute-start(f32[1600,128]{1,0:T(8,128)S(1)} %bitcast.18), channel_id=1, source_target_pairs={{0,4},{4,0},{8,12},{12,8},{1,5},{5,1},{9,13},{13,9},{2,6},{6,2},{1... | collective-permute-start | bytes 2457608 | tf_op jit(solution)/shard_map/ppermute | solution.py:803
  2.0 2.6 %collective-permute-start.2 = (f32[272,128]{1,0:T(8,128)S(1)}, f32[272,128]{1,0:T(8,128)S(1)}, u32[]{:S(2)}, u32[]{:S(2)}) collective-permute-start(f32[272,128]{1,0:T(8,128)S(1)} %get-tuple-element.50), channel_id=1, source_target_pairs={{0,12},{4,8},{8,4},{12,0},{1,13},{5,9},{9,5},{13,1},{2,14},{6,10},... | collective-permute-start | bytes 417800 | tf_op jit(solution)/shard_map/ppermute | solution.py:802
  4.6 0.3 %edge.1 = f32[32,128]{1,0:T(8,128)S(1)} custom-call(f32[1600,128]{1,0:T(8,128)S(1)} %bitcast.19), custom_call_target="tpu_custom_call" | custom-call | flops 1000 | bytes 1000 | tf_op jit(solution)/shard_map/edge/pallas_call | solution.py:804
  4.9 0.0 copy-start.1
  4.9 1.6 %collective-permute-start.1 = (f32[32,128]{1,0:T(8,128)S(1)}, f32[32,128]{1,0:T(8,128)S(1)}, u32[]{:S(2)}, u32[]{:S(2)}) collective-permute-start(f32[32,128]{1,0:T(8,128)S(1)} %edge.1), channel_id=1, source_target_pairs={{0,16},{16,0},{1,17},{17,1},{2,18},{18,2},{3,19},{19,3},{4,20},{20... | collective-permute-start | bytes 49160 | tf_op jit(solution)/shard_map/ppermute | solution.py:805
  6.5 0.0 copy-done
  6.5 0.0 copy-done.1
  6.5 0.7 %factor.1 = (f32[80,4,128]{2,1,0:T(4,128)S(1)}, f32[80,4,128]{2,1,0:T(4,128)S(1)}, f32[80,4,128]{2,1,0:T(4,128)S(1)}, f32[80,4,128]{2,1,0:T(4,128)S(1)}, f32[80,...) custom-call(f32[4,80,4,128]{3,2,1,0:T(4,128)S(1)} %bitcast.22, f32[4,128]{1,0:T(4,128)S(1)} %bitcast.28), custom_call_target="tpu_custom_call" | custom-call | flops 4000000 | bytes 4000000 | tf_op jit(solution)/shard_map/factor/pallas_call | solution.py:811
  7.2 0.8 %element.1 = (f32[1600,128]{1,0:T(8,128)S(1)}, f32[4,88,128]{2,1,0:T(8,128)S(1)}) custom-call(f32[1600,128]{1,0:T(8,128)S(1)} %bitcast.20, s32[4,128]{1,0:T(4,128)S(1)} %get-tuple-element.43.neighbour_face, s32[4,128]{1,0:T(4,128)S(1)} %get-tuple-element.44.orientation, f32[16,128]{1,0:T(8,128)S(1)} %get-tuple-element.46.metric, ...), custom_call_target="tpu_custom_call" | custom-call | flops 4000000 | bytes 4000000 | tf_op jit(solution)/shard_map/element/pallas_call | solution.py:815
  8.0 0.0 collective-permute-done.state
  8.0 0.3 %near.1 = (f32[4,88,128]{2,1,0:T(8,128)S(1)}, f32[320,128]{1,0:T(8,128)S(1)}) custom-call(f32[1600,128]{1,0:T(8,128)S(1)} %collective-permute-done.state, s32[4,128]{1,0:T(4,128)S(1)} %get-tuple-element.43.neighbour_face, s32[4,128]{1,0:T(4,128)S(1)} %get-tuple-element.44.orientation, f32[56,128]{1,0:T(8,128)S(1)} %get-tuple-element.45.fluxes, ...), custom_call_target="tpu_custom_call" | custom-call | flops 1000 | bytes 1000 | tf_op jit(solution)/shard_map/near/pallas_call | solution.py:835
  8.3 0.4 %collective-permute-done.1.from_down.from_up = f32[32,128]{1,0:T(8,128)S(1)} collective-permute-done((f32[32,128]{1,0:T(8,128)S(1)}, f32[32,128]{1,0:T(8,128)S(1)}, u32[]{:S(2)}, u32[]{:S(2)}) %collective-permute-start.1) | collective-permute-done | bytes 16416 | tf_op jit(solution)/shard_map/ppermute | solution.py:805
  8.7 0.2 half_pack.1.half
  9.0 0.0 collective-permute-done.2.from_other.received
  9.0 2.7 %collective-permute-start.3 = (f32[88,128]{1,0:T(8,128)S(1)}, f32[88,128]{1,0:T(8,128)S(1)}, u32[]{:S(2)}, u32[]{:S(2)}) collective-permute-start(f32[88,128]{1,0:T(8,128)S(1)} %get-tuple-element.51), channel_id=1, source_target_pairs={{0,2},{1,3},{2,0},{3,1},{4,6},{5,7},{6,4},{7,5},{8,10},{9,11},{10,... | collective-permute-start | bytes 135176 | tf_op jit(solution)/shard_map/ppermute | solution.py:749
  11.7 1.3 %collective-permute-start.4 = (f32[88,128]{1,0:T(8,128)S(1)}, f32[88,128]{1,0:T(8,128)S(1)}, u32[]{:S(2)}, u32[]{:S(2)}) collective-permute-start(f32[88,128]{1,0:T(8,128)S(1)} %get-tuple-element.52), channel_id=1, source_target_pairs={{0,3},{1,2},{2,1},{3,0},{4,7},{5,6},{6,5},{7,4},{8,11},{9,10},{10,... | collective-permute-start | bytes 135176 | tf_op jit(solution)/shard_map/ppermute | solution.py:749
  13.0 0.2 collective-permute-start.5
  13.3 0.3 other_face.1
  13.5 0.5 %collective-permute-start.9 = (f32[160,128]{1,0:T(8,128)S(1)}, f32[160,128]{1,0:T(8,128)S(1)}, u32[]{:S(2)}, u32[]{:S(2)}) collective-permute-start(f32[160,128]{1,0:T(8,128)S(1)} %get-tuple-element.61), channel_id=1, source_target_pairs={{0,12},{4,8},{8,4},{12,0},{1,13},{5,9},{9,5},{13,1},{2,14},{6,10},... | collective-permute-start | bytes 245768 | tf_op jit(solution)/shard_map/ppermute | solution.py:882
  14.0 1.3 %collective-permute-start.10 = (f32[160,128]{1,0:T(8,128)S(1)}, f32[160,128]{1,0:T(8,128)S(1)}, u32[]{:S(2)}, u32[]{:S(2)}) collective-permute-start(f32[160,128]{1,0:T(8,128)S(1)} %get-tuple-element.62), channel_id=1, source_target_pairs={{0,12},{4,8},{8,4},{12,0},{1,13},{5,9},{9,5},{13,1},{2,14},{6,10},... | collective-permute-start | bytes 245768 | tf_op jit(solution)/shard_map/ppermute | solution.py:882
  15.3 0.0 collective-permute-done.3
  15.3 2.2 %collective-permute-done.4 = f32[88,128]{1,0:T(8,128)S(1)} collective-permute-done((f32[88,128]{1,0:T(8,128)S(1)}, f32[88,128]{1,0:T(8,128)S(1)}, u32[]{:S(2)}, u32[]{:S(2)}) %collective-permute-start.4) | collective-permute-done | bytes 45088 | tf_op jit(solution)/shard_map/ppermute | solution.py:749
  17.6 0.0 collective-permute-done.5
  17.6 0.2 solve.1
  17.8 1.4 %collective-permute-start.7 = (f32[88,128]{1,0:T(8,128)S(1)}, f32[88,128]{1,0:T(8,128)S(1)}, u32[]{:S(2)}, u32[]{:S(2)}) collective-permute-start(f32[88,128]{1,0:T(8,128)S(1)} %bitcast.31), channel_id=1, source_target_pairs={{0,2},{1,3},{2,0},{3,1},{4,6},{5,7},{6,4},{7,5},{8,10},{9,11},{10,... | collective-permute-start | bytes 135176 | tf_op jit(solution)/shard_map/ppermute | solution.py:749
  19.2 1.1 %collective-permute-start.6 = (f32[88,128]{1,0:T(8,128)S(1)}, f32[88,128]{1,0:T(8,128)S(1)}, u32[]{:S(2)}, u32[]{:S(2)}) collective-permute-start(f32[88,128]{1,0:T(8,128)S(1)} %bitcast.30), channel_id=1, source_target_pairs={{0,3},{1,2},{2,1},{3,0},{4,7},{5,6},{6,5},{7,4},{8,11},{9,10},{10,... | collective-permute-start | bytes 135176 | tf_op jit(solution)/shard_map/ppermute | solution.py:749
  20.3 1.1 %collective-permute-start.8 = (f32[88,128]{1,0:T(8,128)S(1)}, f32[88,128]{1,0:T(8,128)S(1)}, u32[]{:S(2)}, u32[]{:S(2)}) collective-permute-start(f32[88,128]{1,0:T(8,128)S(1)} %bitcast.29), channel_id=1, source_target_pairs={{0,1},{1,0},{2,3},{3,2},{4,5},{5,4},{6,7},{7,6},{8,9},{9,8},{10,11... | collective-permute-start | bytes 135176 | tf_op jit(solution)/shard_map/ppermute | solution.py:749
  21.4 0.0 collective-permute-done.9.other_early
  21.4 0.0 collective-permute-done.10.other_late
  21.4 1.3 %finish.1 = (f32[5,320,128]{2,1,0:T(8,128)}, f32[2,320,128]{2,1,0:T(8,128)S(1)}) custom-call(f32[1600,128]{1,0:T(8,128)S(1)} %get-tuple-element.59.part, f32[320,128]{1,0:T(8,128)S(1)} %get-tuple-element.60.near, f32[160,128]{1,0:T(8,128)S(1)} %collective-permute-done.9.other_early, f32[160,128]{1,0:T(8,128)S(1)} %collective-permute-done.10.other_late, ...), custom_call_target="tpu_custom_call" | custom-call | flops 4000000 | bytes 4000000 | tf_op jit(solution)/shard_map/finish/pallas_call | solution.py:900
  22.7 0.6 %collective-permute-done.7.refs_1_ = f32[88,128]{1,0:T(8,128)S(1)} collective-permute-done((f32[88,128]{1,0:T(8,128)S(1)}, f32[88,128]{1,0:T(8,128)S(1)}, u32[]{:S(2)}, u32[]{:S(2)}) %collective-permute-start.7) | collective-permute-done | bytes 45088 | tf_op jit(solution)/shard_map/ppermute | solution.py:749
  23.3 1.7 %collective-permute-done.6.refs_0_ = f32[88,128]{1,0:T(8,128)S(1)} collective-permute-done((f32[88,128]{1,0:T(8,128)S(1)}, f32[88,128]{1,0:T(8,128)S(1)}, u32[]{:S(2)}, u32[]{:S(2)}) %collective-permute-start.6) | collective-permute-done | bytes 45088 | tf_op jit(solution)/shard_map/ppermute | solution.py:749
  25.0 0.0 collective-permute-done.8.refs_2_
  25.0 0.9 %update.1 = f32[5,320,128]{2,1,0:T(8,128)} custom-call(f32[88,128]{1,0:T(8,128)S(1)} %collective-permute-done.6.refs_0_, f32[88,128]{1,0:T(8,128)S(1)} %collective-permute-done.7.refs_1_, f32[88,128]{1,0:T(8,128)S(1)} %collective-permute-done.8.refs_2_, f32[88,128]{1,0:T(8,128)S(1)} %bitcast.24, ...), custom_call_target="tpu_custom_call", output_to_operand_aliasing={{}: (5, {})} | custom-call | tf_op jit(solution)/shard_map/update/pallas_call | solution.py:918
  (1 shorter events, 0.0 us)
Async XLA Ops:
  0.0 6.5 %copy-start = (f32[4,80,1,4,1,128]{5,4,3,2,1,0:T(1,128)S(1)}, f32[4,80,1,4,1,128]{5,4,3,2,1,0:T(1,128)}, u32[]{:S(2)}) copy-start(f32[4,80,1,4,1,128]{5,4,3,2,1,0:T(1,128)} %param.15) | copy-start | bytes 1966084
  1.4 6.6 %collective-permute-start = (f32[1600,128]{1,0:T(8,128)S(1)}, f32[1600,128]{1,0:T(8,128)S(1)}, u32[]{:S(2)}, u32[]{:S(2)}) collective-permute-start(f32[1600,128]{1,0:T(8,128)S(1)} %bitcast.18), channel_id=1, source_target_pairs={{0,4},{4,0},{8,12},{12,8},{1,5},{5,1},{9,13},{13,9},{2,6},{6,2},{1... | collective-permute-start | bytes 2457608 | tf_op jit(solution)/shard_map/ppermute | solution.py:803
  2.0 7.0 %collective-permute-start.2 = (f32[272,128]{1,0:T(8,128)S(1)}, f32[272,128]{1,0:T(8,128)S(1)}, u32[]{:S(2)}, u32[]{:S(2)}) collective-permute-start(f32[272,128]{1,0:T(8,128)S(1)} %get-tuple-element.50), channel_id=1, source_target_pairs={{0,12},{4,8},{8,4},{12,0},{1,13},{5,9},{9,5},{13,1},{2,14},{6,10},... | collective-permute-start | bytes 417800 | tf_op jit(solution)/shard_map/ppermute | solution.py:802
  4.9 1.6 %copy-start.1 = (f32[1,4,1,128]{3,2,1,0:T(1,128)S(1)}, f32[1,4,1,128]{3,2,1,0:T(1,128)}, u32[]{:S(2)}) copy-start(f32[1,4,1,128]{3,2,1,0:T(1,128)} %param.16) | copy-start | bytes 6148
  4.9 3.8 %collective-permute-start.1 = (f32[32,128]{1,0:T(8,128)S(1)}, f32[32,128]{1,0:T(8,128)S(1)}, u32[]{:S(2)}, u32[]{:S(2)}) collective-permute-start(f32[32,128]{1,0:T(8,128)S(1)} %edge.1), channel_id=1, source_target_pairs={{0,16},{16,0},{1,17},{17,1},{2,18},{18,2},{3,19},{19,3},{4,20},{20... | collective-permute-start | bytes 49160 | tf_op jit(solution)/shard_map/ppermute | solution.py:805
  9.0 6.3 %collective-permute-start.3 = (f32[88,128]{1,0:T(8,128)S(1)}, f32[88,128]{1,0:T(8,128)S(1)}, u32[]{:S(2)}, u32[]{:S(2)}) collective-permute-start(f32[88,128]{1,0:T(8,128)S(1)} %get-tuple-element.51), channel_id=1, source_target_pairs={{0,2},{1,3},{2,0},{3,1},{4,6},{5,7},{6,4},{7,5},{8,10},{9,11},{10,... | collective-permute-start | bytes 135176 | tf_op jit(solution)/shard_map/ppermute | solution.py:749
  11.7 5.9 %collective-permute-start.4 = (f32[88,128]{1,0:T(8,128)S(1)}, f32[88,128]{1,0:T(8,128)S(1)}, u32[]{:S(2)}, u32[]{:S(2)}) collective-permute-start(f32[88,128]{1,0:T(8,128)S(1)} %get-tuple-element.52), channel_id=1, source_target_pairs={{0,3},{1,2},{2,1},{3,0},{4,7},{5,6},{6,5},{7,4},{8,11},{9,10},{10,... | collective-permute-start | bytes 135176 | tf_op jit(solution)/shard_map/ppermute | solution.py:749
  13.0 4.5 %collective-permute-start.5 = (f32[88,128]{1,0:T(8,128)S(1)}, f32[88,128]{1,0:T(8,128)S(1)}, u32[]{:S(2)}, u32[]{:S(2)}) collective-permute-start(f32[88,128]{1,0:T(8,128)S(1)} %get-tuple-element.53), channel_id=1, source_target_pairs={{0,1},{1,0},{2,3},{3,2},{4,5},{5,4},{6,7},{7,6},{8,9},{9,8},{10,11... | collective-permute-start | bytes 135176 | tf_op jit(solution)/shard_map/ppermute | solution.py:749
  13.5 7.8 %collective-permute-start.9 = (f32[160,128]{1,0:T(8,128)S(1)}, f32[160,128]{1,0:T(8,128)S(1)}, u32[]{:S(2)}, u32[]{:S(2)}) collective-permute-start(f32[160,128]{1,0:T(8,128)S(1)} %get-tuple-element.61), channel_id=1, source_target_pairs={{0,12},{4,8},{8,4},{12,0},{1,13},{5,9},{9,5},{13,1},{2,14},{6,10},... | collective-permute-start | bytes 245768 | tf_op jit(solution)/shard_map/ppermute | solution.py:882
  14.0 7.4 %collective-permute-start.10 = (f32[160,128]{1,0:T(8,128)S(1)}, f32[160,128]{1,0:T(8,128)S(1)}, u32[]{:S(2)}, u32[]{:S(2)}) collective-permute-start(f32[160,128]{1,0:T(8,128)S(1)} %get-tuple-element.62), channel_id=1, source_target_pairs={{0,12},{4,8},{8,4},{12,0},{1,13},{5,9},{9,5},{13,1},{2,14},{6,10},... | collective-permute-start | bytes 245768 | tf_op jit(solution)/shard_map/ppermute | solution.py:882
  17.8 5.5 %collective-permute-start.7 = (f32[88,128]{1,0:T(8,128)S(1)}, f32[88,128]{1,0:T(8,128)S(1)}, u32[]{:S(2)}, u32[]{:S(2)}) collective-permute-start(f32[88,128]{1,0:T(8,128)S(1)} %bitcast.31), channel_id=1, source_target_pairs={{0,2},{1,3},{2,0},{3,1},{4,6},{5,7},{6,4},{7,5},{8,10},{9,11},{10,... | collective-permute-start | bytes 135176 | tf_op jit(solution)/shard_map/ppermute | solution.py:749
  19.2 5.8 %collective-permute-start.6 = (f32[88,128]{1,0:T(8,128)S(1)}, f32[88,128]{1,0:T(8,128)S(1)}, u32[]{:S(2)}, u32[]{:S(2)}) collective-permute-start(f32[88,128]{1,0:T(8,128)S(1)} %bitcast.30), channel_id=1, source_target_pairs={{0,3},{1,2},{2,1},{3,0},{4,7},{5,6},{6,5},{7,4},{8,11},{9,10},{10,... | collective-permute-start | bytes 135176 | tf_op jit(solution)/shard_map/ppermute | solution.py:749
  20.3 4.7 %collective-permute-start.8 = (f32[88,128]{1,0:T(8,128)S(1)}, f32[88,128]{1,0:T(8,128)S(1)}, u32[]{:S(2)}, u32[]{:S(2)}) collective-permute-start(f32[88,128]{1,0:T(8,128)S(1)} %bitcast.29), channel_id=1, source_target_pairs={{0,1},{1,0},{2,3},{3,2},{4,5},{5,4},{6,7},{7,6},{8,9},{9,8},{10,11... | collective-permute-start | bytes 135176 | tf_op jit(solution)/shard_map/ppermute | solution.py:749

commit v4 on v3

--- a/solution.py
+++ b/solution.py
@@ -668,7 +668,6 @@
         speed[me ^ way] = values[...]
     lanes = done.shape[2]
     half = levels // 2
-    early = (7 * half) // 10
     low = lax.broadcasted_iota(jnp.int32, (ROWS, lanes), 0) < NODES
     copies = []
     for pair in range(half):
@@ -684,8 +683,8 @@
                 final[0, at, :] = done[0, at, :] - density_couple * jumps
                 final[1, at, :] = side_by_side(value[a], value[b], 1 - odd, low)
                 final[2, at, :] = done[1, at, :] - theta_couple * jumps
-        if pair in (early - 1, half - 1):
-            first = 0 if pair < half - 1 else early
+        if pair == half - 1:
+            first = 0
             rows = pl.ds(first * 2 * POINTS, (pair + 1 - first) * 2 * POINTS)
             for place, f, count in ((1, 3, 2), (0, 0, 1)):
                 copies.append(
@@ -924,7 +923,7 @@
         scratch_shapes=[
             pltpu.VMEM((NODES,) + block, jnp.float32),
             pltpu.VMEM((3, size, lanes), jnp.float32),
-            pltpu.SemaphoreType.DMA((4,)),
+            pltpu.SemaphoreType.DMA((2,)),
         ],
         compiler_params=limits,
         name="update",

time: 26.1 us -> 26.1 us (level)
  no operation moved by 1% of the time
where the time goes in v4:
time: 26.1 us; the launch traced here: 25.9 us
  starting transfers between devices  14.3 us (55%)
  Pallas kernels  6.54 us (25%)
  waiting for transfers between devices  4.97 us (19%)
    ppermute x6, starting transfers between devices, exchange(): lax.ppermute(x, 'vz', [(i, i ^ way) for i in range(size)])  7.79 us
    ppermute x6, waiting for transfers between devices, exchange(): lax.ppermute(x, 'vz', [(i, i ^ way) for i in range(size)])  4.58 us
    ppermute x1, starting transfers between devices, per_device(): from_other = lax.ppermute(to_other, 'hy', other)  2.64 us
    ppermute x2, starting transfers between devices, per_device(): other_face = [lax.ppermute(x, 'hy', other) for x in other_face]  1.81 us
    ppermute x1, starting transfers between devices, per_device(): from_down = lax.ppermute(to_sides, 'hx', second_up)  1.56 us
    pallas_call x1, Pallas kernels, per_device(): call(rim_kernel, [message, whole, table, table, (POINTS, lanes), tables.s...  1.44 us
    pallas_call x1, Pallas kernels, per_device(): pl.pallas_call(finish_section_kernel, out_shape=[jax.ShapeDtypeStruct(who...  1.33 us
    pallas_call x1, Pallas kernels, per_device(): pl.pallas_call(update_kernel, out_shape=jax.ShapeDtypeStruct(whole, jnp.f...  0.87 us
  transfers between devices with their start and end apart: 11, of which 4 were waited for; matrix products, arithmetic and copies ran while one was open for 0% of the time, Pallas kernels for 16%

profile of v4, /device:TPU:0, one launch (start us, length us, event | category | flops | bytes accessed | tf_op | source)
XLA Modules:
  0.0 25.9 jit_solution(17303881467565112100)
XLA Ops:
  0.0 0.0 copy-start
  0.0 1.4 %rim.1 = (f32[272,128]{1,0:T(8,128)S(1)}, f32[5,320,128]{2,1,0:T(8,128)S(1)}, s32[4,128]{1,0:T(4,128)S(1)}, s32[4,128]{1,0:T(4,128)S(1)}, f32[16,128]{1,0:T(8,12...) custom-call(f32[5,320,128]{2,1,0:T(8,128)} %bitcast.32, s32[4,128]{1,0:T(4,128)} %bitcast.34, s32[4,128]{1,0:T(4,128)} %bitcast.35, ...), custom_call_target="tpu_custom_call" | custom-call | flops 1000 | bytes 1000 | tf_op jit(solution)/shard_map/rim/pallas_call | solution.py:778
  1.4 0.5 %collective-permute-start = (f32[1600,128]{1,0:T(8,128)S(1)}, f32[1600,128]{1,0:T(8,128)S(1)}, u32[]{:S(2)}, u32[]{:S(2)}) collective-permute-start(f32[1600,128]{1,0:T(8,128)S(1)} %bitcast.18), channel_id=1, source_target_pairs={{0,4},{4,0},{8,12},{12,8},{1,5},{5,1},{9,13},{13,9},{2,6},{6,2},{1... | collective-permute-start | bytes 2457608 | tf_op jit(solution)/shard_map/ppermute | solution.py:802
  2.0 2.6 %collective-permute-start.2 = (f32[272,128]{1,0:T(8,128)S(1)}, f32[272,128]{1,0:T(8,128)S(1)}, u32[]{:S(2)}, u32[]{:S(2)}) collective-permute-start(f32[272,128]{1,0:T(8,128)S(1)} %get-tuple-element.50), channel_id=1, source_target_pairs={{0,12},{4,8},{8,4},{12,0},{1,13},{5,9},{9,5},{13,1},{2,14},{6,10},... | collective-permute-start | bytes 417800 | tf_op jit(solution)/shard_map/ppermute | solution.py:801
  4.6 0.3 %edge.1 = f32[32,128]{1,0:T(8,128)S(1)} custom-call(f32[1600,128]{1,0:T(8,128)S(1)} %bitcast.19), custom_call_target="tpu_custom_call" | custom-call | flops 1000 | bytes 1000 | tf_op jit(solution)/shard_map/edge/pallas_call | solution.py:803
  4.9 0.0 copy-start.1
  4.9 1.6 %collective-permute-start.1 = (f32[32,128]{1,0:T(8,128)S(1)}, f32[32,128]{1,0:T(8,128)S(1)}, u32[]{:S(2)}, u32[]{:S(2)}) collective-permute-start(f32[32,128]{1,0:T(8,128)S(1)} %edge.1), channel_id=1, source_target_pairs={{0,16},{16,0},{1,17},{17,1},{2,18},{18,2},{3,19},{19,3},{4,20},{20... | collective-permute-start | bytes 49160 | tf_op jit(solution)/shard_map/ppermute | solution.py:804
  6.5 0.0 copy-done
  6.5 0.0 copy-done.1
  6.5 0.7 %factor.1 = (f32[80,4,128]{2,1,0:T(4,128)S(1)}, f32[80,4,128]{2,1,0:T(4,128)S(1)}, f32[80,4,128]{2,1,0:T(4,128)S(1)}, f32[80,4,128]{2,1,0:T(4,128)S(1)}, f32[80,...) custom-call(f32[4,80,4,128]{3,2,1,0:T(4,128)S(1)} %bitcast.22, f32[4,128]{1,0:T(4,128)S(1)} %bitcast.28), custom_call_target="tpu_custom_call" | custom-call | flops 4000000 | bytes 4000000 | tf_op jit(solution)/shard_map/factor/pallas_call | solution.py:810
  7.2 0.8 %element.1 = (f32[1600,128]{1,0:T(8,128)S(1)}, f32[4,88,128]{2,1,0:T(8,128)S(1)}) custom-call(f32[1600,128]{1,0:T(8,128)S(1)} %bitcast.20, s32[4,128]{1,0:T(4,128)S(1)} %get-tuple-element.43.neighbour_face, s32[4,128]{1,0:T(4,128)S(1)} %get-tuple-element.44.orientation, f32[16,128]{1,0:T(8,128)S(1)} %get-tuple-element.46.metric, ...), custom_call_target="tpu_custom_call" | custom-call | flops 4000000 | bytes 4000000 | tf_op jit(solution)/shard_map/element/pallas_call | solution.py:814
  8.0 0.0 collective-permute-done.state
  8.0 0.3 %near.1 = (f32[4,88,128]{2,1,0:T(8,128)S(1)}, f32[320,128]{1,0:T(8,128)S(1)}) custom-call(f32[1600,128]{1,0:T(8,128)S(1)} %collective-permute-done.state, s32[4,128]{1,0:T(4,128)S(1)} %get-tuple-element.43.neighbour_face, s32[4,128]{1,0:T(4,128)S(1)} %get-tuple-element.44.orientation, f32[56,128]{1,0:T(8,128)S(1)} %get-tuple-element.45.fluxes, ...), custom_call_target="tpu_custom_call" | custom-call | flops 1000 | bytes 1000 | tf_op jit(solution)/shard_map/near/pallas_call | solution.py:834
  8.3 0.4 %collective-permute-done.1.from_down.from_up = f32[32,128]{1,0:T(8,128)S(1)} collective-permute-done((f32[32,128]{1,0:T(8,128)S(1)}, f32[32,128]{1,0:T(8,128)S(1)}, u32[]{:S(2)}, u32[]{:S(2)}) %collective-permute-start.1) | collective-permute-done | bytes 16416 | tf_op jit(solution)/shard_map/ppermute | solution.py:804
  8.7 0.2 half_pack.1.half
  9.0 0.0 collective-permute-done.2.from_other.received
  9.0 2.7 %collective-permute-start.3 = (f32[88,128]{1,0:T(8,128)S(1)}, f32[88,128]{1,0:T(8,128)S(1)}, u32[]{:S(2)}, u32[]{:S(2)}) collective-permute-start(f32[88,128]{1,0:T(8,128)S(1)} %get-tuple-element.51), channel_id=1, source_target_pairs={{0,2},{1,3},{2,0},{3,1},{4,6},{5,7},{6,4},{7,5},{8,10},{9,11},{10,... | collective-permute-start | bytes 135176 | tf_op jit(solution)/shard_map/ppermute | solution.py:748
  11.7 1.3 %collective-permute-start.4 = (f32[88,128]{1,0:T(8,128)S(1)}, f32[88,128]{1,0:T(8,128)S(1)}, u32[]{:S(2)}, u32[]{:S(2)}) collective-permute-start(f32[88,128]{1,0:T(8,128)S(1)} %get-tuple-element.52), channel_id=1, source_target_pairs={{0,3},{1,2},{2,1},{3,0},{4,7},{5,6},{6,5},{7,4},{8,11},{9,10},{10,... | collective-permute-start | bytes 135176 | tf_op jit(solution)/shard_map/ppermute | solution.py:748
  13.0 0.2 collective-permute-start.5
  13.3 0.3 other_face.1
  13.5 0.5 %collective-permute-start.9 = (f32[160,128]{1,0:T(8,128)S(1)}, f32[160,128]{1,0:T(8,128)S(1)}, u32[]{:S(2)}, u32[]{:S(2)}) collective-permute-start(f32[160,128]{1,0:T(8,128)S(1)} %get-tuple-element.61), channel_id=1, source_target_pairs={{0,12},{4,8},{8,4},{12,0},{1,13},{5,9},{9,5},{13,1},{2,14},{6,10},... | collective-permute-start | bytes 245768 | tf_op jit(solution)/shard_map/ppermute | solution.py:881
  14.0 1.3 %collective-permute-start.10 = (f32[160,128]{1,0:T(8,128)S(1)}, f32[160,128]{1,0:T(8,128)S(1)}, u32[]{:S(2)}, u32[]{:S(2)}) collective-permute-start(f32[160,128]{1,0:T(8,128)S(1)} %get-tuple-element.62), channel_id=1, source_target_pairs={{0,12},{4,8},{8,4},{12,0},{1,13},{5,9},{9,5},{13,1},{2,14},{6,10},... | collective-permute-start | bytes 245768 | tf_op jit(solution)/shard_map/ppermute | solution.py:881
  15.3 0.0 collective-permute-done.3
  15.3 2.2 %collective-permute-done.4 = f32[88,128]{1,0:T(8,128)S(1)} collective-permute-done((f32[88,128]{1,0:T(8,128)S(1)}, f32[88,128]{1,0:T(8,128)S(1)}, u32[]{:S(2)}, u32[]{:S(2)}) %collective-permute-start.4) | collective-permute-done | bytes 45088 | tf_op jit(solution)/shard_map/ppermute | solution.py:748
  17.6 0.0 collective-permute-done.5
  17.6 0.2 solve.1
  17.8 1.4 %collective-permute-start.7 = (f32[88,128]{1,0:T(8,128)S(1)}, f32[88,128]{1,0:T(8,128)S(1)}, u32[]{:S(2)}, u32[]{:S(2)}) collective-permute-start(f32[88,128]{1,0:T(8,128)S(1)} %bitcast.31), channel_id=1, source_target_pairs={{0,2},{1,3},{2,0},{3,1},{4,6},{5,7},{6,4},{7,5},{8,10},{9,11},{10,... | collective-permute-start | bytes 135176 | tf_op jit(solution)/shard_map/ppermute | solution.py:748
  19.2 1.1 %collective-permute-start.6 = (f32[88,128]{1,0:T(8,128)S(1)}, f32[88,128]{1,0:T(8,128)S(1)}, u32[]{:S(2)}, u32[]{:S(2)}) collective-permute-start(f32[88,128]{1,0:T(8,128)S(1)} %bitcast.30), channel_id=1, source_target_pairs={{0,3},{1,2},{2,1},{3,0},{4,7},{5,6},{6,5},{7,4},{8,11},{9,10},{10,... | collective-permute-start | bytes 135176 | tf_op jit(solution)/shard_map/ppermute | solution.py:748
  20.3 1.1 %collective-permute-start.8 = (f32[88,128]{1,0:T(8,128)S(1)}, f32[88,128]{1,0:T(8,128)S(1)}, u32[]{:S(2)}, u32[]{:S(2)}) collective-permute-start(f32[88,128]{1,0:T(8,128)S(1)} %bitcast.29), channel_id=1, source_target_pairs={{0,1},{1,0},{2,3},{3,2},{4,5},{5,4},{6,7},{7,6},{8,9},{9,8},{10,11... | collective-permute-start | bytes 135176 | tf_op jit(solution)/shard_map/ppermute | solution.py:748
  21.4 0.0 collective-permute-done.9.other_early
  21.4 0.0 collective-permute-done.10.other_late
  21.4 1.3 %finish.1 = (f32[5,320,128]{2,1,0:T(8,128)}, f32[2,320,128]{2,1,0:T(8,128)S(1)}) custom-call(f32[1600,128]{1,0:T(8,128)S(1)} %get-tuple-element.59.part, f32[320,128]{1,0:T(8,128)S(1)} %get-tuple-element.60.near, f32[160,128]{1,0:T(8,128)S(1)} %collective-permute-done.9.other_early, f32[160,128]{1,0:T(8,128)S(1)} %collective-permute-done.10.other_late, ...), custom_call_target="tpu_custom_call" | custom-call | flops 4000000 | bytes 4000000 | tf_op jit(solution)/shard_map/finish/pallas_call | solution.py:899
  22.7 0.6 %collective-permute-done.7.refs_1_ = f32[88,128]{1,0:T(8,128)S(1)} collective-permute-done((f32[88,128]{1,0:T(8,128)S(1)}, f32[88,128]{1,0:T(8,128)S(1)}, u32[]{:S(2)}, u32[]{:S(2)}) %collective-permute-start.7) | collective-permute-done | bytes 45088 | tf_op jit(solution)/shard_map/ppermute | solution.py:748
  23.3 1.7 %collective-permute-done.6.refs_0_ = f32[88,128]{1,0:T(8,128)S(1)} collective-permute-done((f32[88,128]{1,0:T(8,128)S(1)}, f32[88,128]{1,0:T(8,128)S(1)}, u32[]{:S(2)}, u32[]{:S(2)}) %collective-permute-start.6) | collective-permute-done | bytes 45088 | tf_op jit(solution)/shard_map/ppermute | solution.py:748
  25.0 0.0 collective-permute-done.8.refs_2_
  25.0 0.9 %update.1 = f32[5,320,128]{2,1,0:T(8,128)} custom-call(f32[88,128]{1,0:T(8,128)S(1)} %collective-permute-done.6.refs_0_, f32[88,128]{1,0:T(8,128)S(1)} %collective-permute-done.7.refs_1_, f32[88,128]{1,0:T(8,128)S(1)} %collective-permute-done.8.refs_2_, f32[88,128]{1,0:T(8,128)S(1)} %bitcast.24, ...), custom_call_target="tpu_custom_call", output_to_operand_aliasing={{}: (5, {})} | custom-call | tf_op jit(solution)/shard_map/update/pallas_call | solution.py:917
  (1 shorter events, 0.0 us)
Async XLA Ops:
  0.0 6.5 %copy-start = (f32[4,80,1,4,1,128]{5,4,3,2,1,0:T(1,128)S(1)}, f32[4,80,1,4,1,128]{5,4,3,2,1,0:T(1,128)}, u32[]{:S(2)}) copy-start(f32[4,80,1,4,1,128]{5,4,3,2,1,0:T(1,128)} %param.15) | copy-start | bytes 1966084
  1.4 6.6 %collective-permute-start = (f32[1600,128]{1,0:T(8,128)S(1)}, f32[1600,128]{1,0:T(8,128)S(1)}, u32[]{:S(2)}, u32[]{:S(2)}) collective-permute-start(f32[1600,128]{1,0:T(8,128)S(1)} %bitcast.18), channel_id=1, source_target_pairs={{0,4},{4,0},{8,12},{12,8},{1,5},{5,1},{9,13},{13,9},{2,6},{6,2},{1... | collective-permute-start | bytes 2457608 | tf_op jit(solution)/shard_map/ppermute | solution.py:802
  2.0 7.0 %collective-permute-start.2 = (f32[272,128]{1,0:T(8,128)S(1)}, f32[272,128]{1,0:T(8,128)S(1)}, u32[]{:S(2)}, u32[]{:S(2)}) collective-permute-start(f32[272,128]{1,0:T(8,128)S(1)} %get-tuple-element.50), channel_id=1, source_target_pairs={{0,12},{4,8},{8,4},{12,0},{1,13},{5,9},{9,5},{13,1},{2,14},{6,10},... | collective-permute-start | bytes 417800 | tf_op jit(solution)/shard_map/ppermute | solution.py:801
  4.9 1.6 %copy-start.1 = (f32[1,4,1,128]{3,2,1,0:T(1,128)S(1)}, f32[1,4,1,128]{3,2,1,0:T(1,128)}, u32[]{:S(2)}) copy-start(f32[1,4,1,128]{3,2,1,0:T(1,128)} %param.16) | copy-start | bytes 6148
  4.9 3.8 %collective-permute-start.1 = (f32[32,128]{1,0:T(8,128)S(1)}, f32[32,128]{1,0:T(8,128)S(1)}, u32[]{:S(2)}, u32[]{:S(2)}) collective-permute-start(f32[32,128]{1,0:T(8,128)S(1)} %edge.1), channel_id=1, source_target_pairs={{0,16},{16,0},{1,17},{17,1},{2,18},{18,2},{3,19},{19,3},{4,20},{20... | collective-permute-start | bytes 49160 | tf_op jit(solution)/shard_map/ppermute | solution.py:804
  9.0 6.3 %collective-permute-start.3 = (f32[88,128]{1,0:T(8,128)S(1)}, f32[88,128]{1,0:T(8,128)S(1)}, u32[]{:S(2)}, u32[]{:S(2)}) collective-permute-start(f32[88,128]{1,0:T(8,128)S(1)} %get-tuple-element.51), channel_id=1, source_target_pairs={{0,2},{1,3},{2,0},{3,1},{4,6},{5,7},{6,4},{7,5},{8,10},{9,11},{10,... | collective-permute-start | bytes 135176 | tf_op jit(solution)/shard_map/ppermute | solution.py:748
  11.7 5.9 %collective-permute-start.4 = (f32[88,128]{1,0:T(8,128)S(1)}, f32[88,128]{1,0:T(8,128)S(1)}, u32[]{:S(2)}, u32[]{:S(2)}) collective-permute-start(f32[88,128]{1,0:T(8,128)S(1)} %get-tuple-element.52), channel_id=1, source_target_pairs={{0,3},{1,2},{2,1},{3,0},{4,7},{5,6},{6,5},{7,4},{8,11},{9,10},{10,... | collective-permute-start | bytes 135176 | tf_op jit(solution)/shard_map/ppermute | solution.py:748
  13.0 4.5 %collective-permute-start.5 = (f32[88,128]{1,0:T(8,128)S(1)}, f32[88,128]{1,0:T(8,128)S(1)}, u32[]{:S(2)}, u32[]{:S(2)}) collective-permute-start(f32[88,128]{1,0:T(8,128)S(1)} %get-tuple-element.53), channel_id=1, source_target_pairs={{0,1},{1,0},{2,3},{3,2},{4,5},{5,4},{6,7},{7,6},{8,9},{9,8},{10,11... | collective-permute-start | bytes 135176 | tf_op jit(solution)/shard_map/ppermute | solution.py:748
  13.5 7.8 %collective-permute-start.9 = (f32[160,128]{1,0:T(8,128)S(1)}, f32[160,128]{1,0:T(8,128)S(1)}, u32[]{:S(2)}, u32[]{:S(2)}) collective-permute-start(f32[160,128]{1,0:T(8,128)S(1)} %get-tuple-element.61), channel_id=1, source_target_pairs={{0,12},{4,8},{8,4},{12,0},{1,13},{5,9},{9,5},{13,1},{2,14},{6,10},... | collective-permute-start | bytes 245768 | tf_op jit(solution)/shard_map/ppermute | solution.py:881
  14.0 7.4 %collective-permute-start.10 = (f32[160,128]{1,0:T(8,128)S(1)}, f32[160,128]{1,0:T(8,128)S(1)}, u32[]{:S(2)}, u32[]{:S(2)}) collective-permute-start(f32[160,128]{1,0:T(8,128)S(1)} %get-tuple-element.62), channel_id=1, source_target_pairs={{0,12},{4,8},{8,4},{12,0},{1,13},{5,9},{9,5},{13,1},{2,14},{6,10},... | collective-permute-start | bytes 245768 | tf_op jit(solution)/shard_map/ppermute | solution.py:881
  17.8 5.5 %collective-permute-start.7 = (f32[88,128]{1,0:T(8,128)S(1)}, f32[88,128]{1,0:T(8,128)S(1)}, u32[]{:S(2)}, u32[]{:S(2)}) collective-permute-start(f32[88,128]{1,0:T(8,128)S(1)} %bitcast.31), channel_id=1, source_target_pairs={{0,2},{1,3},{2,0},{3,1},{4,6},{5,7},{6,4},{7,5},{8,10},{9,11},{10,... | collective-permute-start | bytes 135176 | tf_op jit(solution)/shard_map/ppermute | solution.py:748
  19.2 5.8 %collective-permute-start.6 = (f32[88,128]{1,0:T(8,128)S(1)}, f32[88,128]{1,0:T(8,128)S(1)}, u32[]{:S(2)}, u32[]{:S(2)}) collective-permute-start(f32[88,128]{1,0:T(8,128)S(1)} %bitcast.30), channel_id=1, source_target_pairs={{0,3},{1,2},{2,1},{3,0},{4,7},{5,6},{6,5},{7,4},{8,11},{9,10},{10,... | collective-permute-start | bytes 135176 | tf_op jit(solution)/shard_map/ppermute | solution.py:748
  20.3 4.7 %collective-permute-start.8 = (f32[88,128]{1,0:T(8,128)S(1)}, f32[88,128]{1,0:T(8,128)S(1)}, u32[]{:S(2)}, u32[]{:S(2)}) collective-permute-start(f32[88,128]{1,0:T(8,128)S(1)} %bitcast.29), channel_id=1, source_target_pairs={{0,1},{1,0},{2,3},{3,2},{4,5},{5,4},{6,7},{7,6},{8,9},{9,8},{10,11... | collective-permute-start | bytes 135176 | tf_op jit(solution)/shard_map/ppermute | solution.py:748
